TPU v7x, 512 devices: a whole 4x4x16 slice. The times are simulated.
512 devices in a mesh: tm: 32 (over x, z_lo), seq: 16 (over y, z_hi, core).
Axes of the slice: x: 4, y: 4, z: 16 (z_hi: 2, z_lo: 8; z = z_hi * 8 + z_lo), core: 2. Of those that a mesh axis runs over, the one named last changes fastest.
Arguments:
- x_start: float32 [2048, 64], P('seq')
- old_states: float32 [32, 2048, 64], P('tm', 'seq')
- hidden: bfloat16 [32, 2048, 2560], P('tm', 'seq')
- modulation: float32 [51, 2, 2560], replicated, may hold values from -4 to 4
- step_index: int32 [32], replicated, may hold values from 0 to 49, as said below
- sigma_table: float32 [51], replicated, may hold values from 0 to 1, as said below
- w_query: bfloat16 [2560, 2048], P(None, 'seq')
- w_key: bfloat16 [2560, 2048], P(None, 'seq')
- w_value: bfloat16 [2560, 2048], P(None, 'seq'), may hold values from -0.125 to 0.125
- qk_gain: float32 [2, 2048], P(None, 'seq'), may hold values from 0.8 to 7.2
- w_head: bfloat16 [2048, 64], replicated, may hold values from -0.5 to 0.5
- w_skip: bfloat16 [2560, 64], replicated, may hold values from -0.125 to 0.125
Outputs:
- drift: float32 [32, 2048, 64], P('tm', 'seq')
- new_states: float32 [32, 2048, 64], P('tm', 'seq')
- error: float32 [32], P('tm')
Inputs may be any that keep to these rules, and one draw needn't show every extreme that they name: `step_index`: strictly increasing; the first is 0 and the last 49. `sigma_table`: falls from step to step.
All inputs are finite; a program needn't handle non-finite values.
Results may differ from a plain program's by a relative error of at most 0.009.
Values may be sent and summed in bfloat16 or wider, within the bound.
No kernel may reach another device: no remote copies, remote signals or barrier semaphores. Data moves between devices by JAX's collectives and lax.ppermute only.
A program may use at most 64 MiB of HBM per device.

v0:
```python
import math

import jax
import jax.numpy as jnp
from jax import lax
from jax.sharding import PartitionSpec as P

HD = 64


def entering(shard, axis, join, neutral):
    place = lax.axis_index(axis)
    gathered = lax.all_gather(shard.astype(jnp.bfloat16), axis)
    state = jnp.zeros_like(shard) + jnp.asarray(neutral, shard.dtype)

    def one(step, state):
        return join(state, lax.dynamic_index_in_dim(gathered, step, 0, False).astype(shard.dtype))

    return lax.fori_loop(0, place, one, state)


def layer_norm(token_rows):
    average = jnp.mean(token_rows, axis=-1, keepdims=True)
    centred = token_rows - average
    spread = jnp.mean(centred * centred, axis=-1, keepdims=True)
    return centred * lax.rsqrt(spread + 1e-06)


def add_terms(earlier, later):
    return earlier + later


def per_device(
    x_start,
    old_states,
    hidden,
    modulation,
    step_index,
    sigma_table,
    w_query,
    w_key,
    w_value,
    qk_gain,
    w_head,
    w_skip,
):
    seq_count = lax.axis_size("seq")
    time_rank = lax.axis_index("tm")
    own_rows = hidden.shape[1]
    feature_count = hidden.shape[2]
    local_cols = w_query.shape[1]
    local_heads = local_cols // HD
    all_cols = local_cols * seq_count
    table_rows = sigma_table.shape[0]
    picker = (jnp.arange(step_index.shape[0]) == time_rank).astype(jnp.int32)
    step_now = jnp.sum(picker * step_index)
    following = jnp.concatenate([step_index[1:], step_index[-1:] + 1])
    step_next = jnp.sum(picker * following)
    table_pos = jnp.arange(table_rows)
    sigma_now = jnp.sum(jnp.where(table_pos == step_now, sigma_table, 0.0))
    sigma_next = jnp.sum(jnp.where(table_pos == step_next, sigma_table, 0.0))
    delta = sigma_next - sigma_now
    row_pick = (table_pos == step_now).astype(jnp.float32)
    mod_now = jnp.dot(
        row_pick[None],
        modulation.reshape(table_rows, 2 * feature_count),
        precision=lax.Precision.HIGHEST,
    ).reshape(2, feature_count)
    scale_row = 1.0 + mod_now[0]
    shift_row = mod_now[1]
    own_normed = (layer_norm(hidden[0].astype(jnp.float32)) * scale_row + shift_row).astype(
        jnp.bfloat16
    )
    joined_weights = jnp.concatenate([w_query, w_key, w_value], axis=1)
    projected = jnp.dot(
        lax.all_gather(own_normed, "seq", axis=0, tiled=True),
        joined_weights,
        preferred_element_type=jnp.float32,
    )
    all_tokens = projected.shape[0]
    query = projected[:, :local_cols]
    key_proj = projected[:, local_cols : 2 * local_cols]
    value_proj = projected[:, 2 * local_cols :]
    query_power, key_power = lax.psum(
        (jnp.sum(query * query, axis=1), jnp.sum(key_proj * key_proj, axis=1)), "seq"
    )
    query_unit = (query * lax.rsqrt(query_power[:, None] / all_cols + 1e-06) * qk_gain[0]).astype(
        jnp.bfloat16
    )
    key_unit = (key_proj * lax.rsqrt(key_power[:, None] / all_cols + 1e-06) * qk_gain[1]).astype(
        jnp.bfloat16
    )
    value_unit = value_proj.astype(jnp.bfloat16)
    key_heads = key_unit.reshape(all_tokens, local_heads, HD)
    value_heads = value_unit.reshape(all_tokens, local_heads, HD)
    block_rows = math.gcd(all_tokens, 512)

    def attend_block(first_row):
        query_block = lax.dynamic_slice_in_dim(query_unit, first_row, block_rows, 0).reshape(
            block_rows, local_heads, HD
        )
        scores = jnp.einsum(
            "qhd,khd->hqk", query_block, key_heads, preferred_element_type=jnp.float32
        ) * HD ** (-0.5)
        highest = jnp.max(scores, axis=-1, keepdims=True)
        raised = jnp.exp(scores - highest)
        summed = jnp.sum(raised, axis=-1)
        output = jnp.einsum(
            "hqk,khd->qhd",
            raised.astype(jnp.bfloat16),
            value_heads,
            preferred_element_type=jnp.float32,
        )
        output = output / jnp.transpose(summed)[:, :, None]
        return output.reshape(block_rows, local_cols).astype(jnp.bfloat16)

    block_starts = jnp.arange(all_tokens // block_rows, dtype=jnp.int32) * block_rows
    attended = lax.map(attend_block, block_starts).reshape(all_tokens, local_cols)
    token_heads = lax.all_to_all(attended, "seq", split_axis=0, concat_axis=1, tiled=True)
    drift_attn = jnp.dot(token_heads, w_head, preferred_element_type=jnp.float32)
    drift = drift_attn + jnp.dot(own_normed, w_skip, preferred_element_type=jnp.float32)
    increment = delta * drift
    earlier_sum = entering(increment, "tm", add_terms, jnp.zeros_like(increment))
    new_state = x_start + (earlier_sum + increment)
    change = new_state - old_states[0]
    change_total = lax.psum(jnp.sum(change * change), "seq")
    error = (change_total / (own_rows * seq_count * change.shape[1])).reshape(1)
    return (drift[None], new_state[None], error)


def solution(mesh):
    return jax.shard_map(
        per_device,
        mesh=mesh,
        in_specs=(
            P("seq", None),
            P("tm", "seq", None),
            P("tm", "seq", None),
            P(),
            P(),
            P(),
            P(None, "seq"),
            P(None, "seq"),
            P(None, "seq"),
            P(None, "seq"),
            P(),
            P(),
        ),
        out_specs=(P("tm", "seq", None), P("tm", "seq", None), P("tm")),
        check_vma=False,
    )
```

profile of v0, /device:TPU:1, one launch (start us, length us, event | category | flops | bytes accessed | tf_op | source)
XLA Modules:
  0.0 618.5 jit_solution(8342241350783497669)
XLA Ops:
  9.3 1.6 pad.5
  15.7 206.7 %all-gather.3.cloned.1.call-done = bf16[2048,2560]{1,0:T(8,128)(2,1)} async-done(((bf16[128,2560]{1,0:T(8,128)(2,1)}), bf16[2048,2560]{1,0:T(8,128)(2,1)}) %all-gather.3.cloned.1.call-update) | async-done | bytes 10485776 | tf_op jit(solution)/shard_map/all_gather | solution.py:76
  222.5 7.0 %fusion.14 = f32[2048,384]{0,1:T(8,128)S(1)} fusion(bf16[2048,2560]{1,0:T(8,128)(2,1)} %all-gather.3.cloned.1.call-done, bf16[2560,128]{1,0:T(8,128)(2,1)S(1)} %copy-done.11, bf16[2560,128]{1,0:T(8,128)(2,1)S(1)} %copy-done.12, bf16[2560,128]{1,0:T(8,128)(2,1)S(1)} %copy-done.13), kind=kOutput, calls=%fused_computation.12 | convolution fusion | flops 4032430080 | bytes 15597568 | tf_op jit(solution)/shard_map/dot_general | solution.py:75
  229.7 1.5 copy-done.1
  231.2 109.9 %all-reduce = (f32[2048]{0:T(1024)S(1)}, f32[2048]{0:T(1024)S(1)}) all-reduce(f32[2048]{0:T(1024)S(1)} %get-tuple-element.69, f32[2048]{0:T(1024)S(1)} %get-tuple-element.68), channel_id=1, replica_groups=mesh['tm'=32,'seq'=16] {'seq'}, use_global_device_ids=true, to_apply=%region_4.5 | all-reduce | flops 4096 | bytes 32768 | tf_op jit(solution)/shard_map/psum | solution.py:84
  341.2 1.8 multiply_convert_fusion
  343.0 33.3 %while.20 = (s32[]{:T(128)}, bf16[4,512,128]{2,1,0:T(8,128)(2,1)}, s32[4]{0:T(128)S(1)}, bf16[2048,128]{0,1:T(8,128)(2,1)S(1)}, bf16[2048,2,64]{0,2,1:T(8,128)(2...) while((s32[]{:T(128)}, bf16[4,512,128]{2,1,0:T(8,128)(2,1)}, ...), condition=%wide.region_10.11_spmd, body=%wide.region_7.10_spmd.sunk | while | flops 553777152 | bytes 27283612 | solution.py:118
  345.9 1.4 multiply_reduce_fusion.4
  347.3 1.6 fusion.59
  348.9 1.6 fusion.60
  354.2 1.4 multiply_reduce_fusion.4
  355.6 1.6 fusion.59
  357.2 1.6 fusion.60
  362.5 1.4 multiply_reduce_fusion.4
  363.9 1.6 fusion.59
  365.6 1.6 fusion.60
  370.9 1.4 multiply_reduce_fusion.4
  372.2 1.6 fusion.59
  373.9 1.7 fusion.60
  376.3 16.6 %all-to-all-start = ((bf16[16,128,128]{2,1,0:T(8,128)(2,1)}), bf16[16,128,128]{2,1,0:T(8,128)(2,1)S(1)}, u32[]{:S(2)}, u32[]{:S(2)}) async-start(bf16[16,128,128]{2,1,0:T(8,128)(2,1)} %bitcast.13), calls=%async_computation | async-start | bytes 1048576 | tf_op jit(solution)/shard_map/all_to_all | solution.py:119
  392.9 1.9 fusion.35
  396.4 15.1 %all-to-all-done = bf16[16,128,128]{2,1,0:T(8,128)(2,1)S(1)} async-done(((bf16[16,128,128]{2,1,0:T(8,128)(2,1)}), bf16[16,128,128]{2,1,0:T(8,128)(2,1)S(1)}, u32[]{:S(2)}, u32[]{:S(2)}) %all-to-all-start) | async-done | bytes 524320 | tf_op jit(solution)/shard_map/all_to_all | solution.py:119
  412.1 119.4 %all-gather = bf16[4096,64]{0,1:T(8,128)(2,1)S(1)} all-gather(bf16[128,64]{0,1:T(8,128)(2,1)S(1)} %get-tuple-element.104), channel_id=2, replica_groups=mesh['tm'=32,'seq'=16] {'tm'}, dimensions={0}, use_global_device_ids=true | all-gather | bytes 540672 | tf_op jit(solution)/shard_map/all_gather | solution.py:13
  533.2 76.6 %psum.23 = f32[]{:T(128)} all-reduce(f32[]{:T(128)} %get-tuple-element.94), channel_id=1, replica_groups=mesh['tm'=32,'seq'=16] {'seq'}, use_global_device_ids=true, to_apply=%region_17.18 | all-reduce | flops 1 | bytes 8 | tf_op jit(solution)/shard_map/psum | solution.py:126
  (71 shorter events, 15.2 us)
Async XLA Ops:
  7.2 388.9 %copy-start = (bf16[2560,64]{0,1:T(8,128)(2,1)S(1)}, bf16[2560,64]{0,1:T(8,128)(2,1)}, u32[]{:S(2)}) copy-start(bf16[2560,64]{0,1:T(8,128)(2,1)} %param.27) | copy-start | bytes 983044
  7.2 4.8 copy-start.10
  7.2 6.6 %copy-start.2 = (bf16[1,128,2560]{2,1,0:T(8,128)(2,1)S(1)}, bf16[1,128,2560]{2,1,0:T(8,128)(2,1)}, u32[]{:S(2)}) copy-start(bf16[1,128,2560]{2,1,0:T(8,128)(2,1)} %param.18) | copy-start | bytes 1966084
  7.2 215.2 %all-gather.3.cloned.1.call-start = ((), (), s32[]{:S(2)}) async-start(), calls=%async_computation.1 | async-start | bytes 11141120 | tf_op jit(solution)/shard_map/all_gather | solution.py:76
  10.9 4.8 copy-start.8
  10.9 211.5 %copy-start.11 = (bf16[2560,128]{1,0:T(8,128)(2,1)S(1)}, bf16[2560,128]{1,0:T(8,128)(2,1)}, u32[]{:S(2)}) copy-start(bf16[2560,128]{1,0:T(8,128)(2,1)} %param.24) | copy-start | bytes 1966084
  10.9 211.5 %copy-start.12 = (bf16[2560,128]{1,0:T(8,128)(2,1)S(1)}, bf16[2560,128]{1,0:T(8,128)(2,1)}, u32[]{:S(2)}) copy-start(bf16[2560,128]{1,0:T(8,128)(2,1)} %param.23) | copy-start | bytes 1966084
  10.9 211.5 %copy-start.13 = (bf16[2560,128]{1,0:T(8,128)(2,1)S(1)}, bf16[2560,128]{1,0:T(8,128)(2,1)}, u32[]{:S(2)}) copy-start(bf16[2560,128]{1,0:T(8,128)(2,1)} %param.22) | copy-start | bytes 1966084
  229.5 1.7 copy-start.1
  343.0 50.0 %copy-start.9 = (f32[51]{0:T(128)S(1)}, f32[51]{0:T(128)}, u32[]{:S(2)}) copy-start(f32[51]{0:T(128)} %param.21) | copy-start | bytes 616
  343.0 53.1 %copy-start.3 = (bf16[128,2560]{1,0:T(8,128)(2,1)S(1)}, bf16[128,2560]{1,0:T(8,128)(2,1)}, u32[]{:S(2)}) copy-start(bf16[128,2560]{1,0:T(8,128)(2,1)} %fusion.26) | copy-start | bytes 1966084
  343.0 68.8 %copy-start.4 = (bf16[2048,64]{0,1:T(8,128)(2,1)S(1)}, bf16[2048,64]{0,1:T(8,128)(2,1)}, u32[]{:S(2)}) copy-start(bf16[2048,64]{0,1:T(8,128)(2,1)} %param.26) | copy-start | bytes 786436
  376.3 155.7 %copy-start.6 = (f32[1,128,64]{1,2,0:T(8,128)S(1)}, f32[1,128,64]{1,2,0:T(8,128)}, u32[]{:S(2)}) copy-start(f32[1,128,64]{1,2,0:T(8,128)} %param.17) | copy-start | bytes 98308
  376.3 155.7 %copy-start.7 = (f32[128,64]{0,1:T(8,128)S(1)}, f32[128,64]{0,1:T(8,128)}, u32[]{:S(2)}) copy-start(f32[128,64]{0,1:T(8,128)} %param.16) | copy-start | bytes 98308
  376.3 35.2 %all-to-all-start = ((bf16[16,128,128]{2,1,0:T(8,128)(2,1)}), bf16[16,128,128]{2,1,0:T(8,128)(2,1)S(1)}, u32[]{:S(2)}, u32[]{:S(2)}) async-start(bf16[16,128,128]{2,1,0:T(8,128)(2,1)} %bitcast.13), calls=%async_computation | async-start | bytes 1048576 | tf_op jit(solution)/shard_map/all_to_all | solution.py:119
  412.0 198.4 %copy-start.5 = (f32[128,64]{0,1:T(8,128)}, f32[128,64]{0,1:T(8,128)S(1)}, u32[]{:S(2)}) copy-start(f32[128,64]{0,1:T(8,128)S(1)} %get-tuple-element.105) | copy-start | bytes 98308
Sparse Core Ops, SparseCore 0:
  15.8 206.5 all-gather.2
where the time goes:
time: 620 us; the launch traced here: 618 us
  blocking collectives  306 us (49%)
  waiting for transfers between devices  222 us (36%)
  matrix products  20.9 us (3%)
  between operations  18.1 us (3%)
  starting transfers between devices  16.6 us (3%)
  other arithmetic  14.3 us (2%)
  local copies, waits for them, and re-layouts  12.5 us (2%)
  loops' own time  8.42 us (1%)
    all_gather x1, waiting for transfers between devices, per_device(): lax.all_gather(own_normed, 'seq', axis=0, tiled=True)  207 us
    all_gather x1, blocking collectives, entering(): gathered = lax.all_gather(shard.astype(jnp.bfloat16), axis)  119 us
    psum x1, blocking collectives, per_device(): lax.psum((jnp.sum(query * query, axis=1), jnp.sum(key_proj * key_proj, ax...  110 us
    psum x1, blocking collectives, per_device(): change_total = lax.psum(jnp.sum(change * change), 'seq')  76.6 us
    all_to_all x1, starting transfers between devices, per_device(): lax.all_to_all(attended, 'seq', split_axis=0, concat_axis=1, tiled=True)  16.6 us
    all_to_all x1, waiting for transfers between devices, per_device(): lax.all_to_all(attended, 'seq', split_axis=0, concat_axis=1, tiled=True)  15.1 us
  transfers between devices with their start and end apart: 2, of which 2 were waited for; matrix products, arithmetic and copies ran while one was open for 0% of the time, Pallas kernels for 0%

commit v1 on v0

v1 whole, which is shorter than its diff:
```python
import functools
import math

import jax
import jax.numpy as jnp
from jax import lax
from jax.experimental import pallas as pl
from jax.experimental.pallas import tpu as pltpu
from jax.sharding import PartitionSpec as P

HD = 64
Y, Z, C = 4, 2, 2
ZL = 8
OFFSETS = (0, -1, 1, 2)
CHUNKS = ((0, 64), (64, 128))


def seq_perm(move):
    pairs = []
    for s in range(Y * Z * C):
        y, z, c = s // (Z * C), (s // C) % Z, s % C
        y, z, c = move(y, z, c)
        pairs.append((s, ((y % Y) * Z + z) * C + c))
    return pairs


TO_CORE = seq_perm(lambda y, z, c: (y, z, 1 - c))
TO_UP = seq_perm(lambda y, z, c: (y + 1, z, c))
TO_DOWN = seq_perm(lambda y, z, c: (y - 1, z, c))
TO_FAR = seq_perm(lambda y, z, c: (y, 1 - z, c))


def along_y(rows):
    half = rows.shape[0] // 2
    below = lax.ppermute(rows, "seq", TO_UP)
    above = lax.ppermute(rows, "seq", TO_DOWN)
    opposite = (
        lax.ppermute(below[:half], "seq", TO_UP),
        lax.ppermute(above[half:], "seq", TO_DOWN),
    )
    return (rows, below, above) + opposite


def project_kernel(
    place_ref, scale_ref, shift_ref, w_ref, own_ref, below_ref, above_ref, first_ref, second_ref,
    mine_ref, other_ref, power_ref, normed_ref,
):
    count = own_ref.shape[0]
    spots = (
        (own_ref, 0), (below_ref, count), (above_ref, 2 * count),
        (first_ref, 3 * count), (second_ref, 3 * count + count // 2),
    )
    scale = 1.0 + scale_ref[...]
    shift = shift_ref[...]
    for ref, start in spots:
        rows = ref[...].astype(jnp.float32)
        average = jnp.mean(rows, axis=-1, keepdims=True)
        centred = rows - average
        spread = jnp.mean(centred * centred, axis=-1, keepdims=True)
        normed = centred * lax.rsqrt(spread + 1e-6) * scale + shift
        normed_ref[start : start + ref.shape[0], :] = normed.astype(jnp.bfloat16)
    normed = normed_ref[...]
    ones = jnp.ones((8, 256), jnp.float32)
    for part in range(3):
        wide = jnp.dot(
            normed, w_ref[:, part * 256 : (part + 1) * 256], preferred_element_type=jnp.float32
        )
        narrow = wide.astype(jnp.bfloat16).reshape(Y, count, 256)
        mine_ref[:, :, part * 128 : (part + 1) * 128] = narrow[:, :, :128]
        other_ref[:, :, part * 128 : (part + 1) * 128] = narrow[:, :, 128:]
        if part < 2:
            for slot, offset in enumerate(OFFSETS):
                block = wide[slot * count : (slot + 1) * count]
                sums = lax.dot_general(
                    ones, block * block, (((1,), (1,)), ((), ())),
                    precision=lax.Precision.HIGHEST, preferred_element_type=jnp.float32,
                )
                target = lax.rem(place_ref[0] + (offset + Y), Y)
                power_ref[target, part : part + 1, :] = sums[:1]


def project(place, scale, shift, weights, pieces):
    count = pieces[0].shape[0]
    features = weights.shape[0]
    vmem = pl.BlockSpec(memory_space=pltpu.VMEM)
    return pl.pallas_call(
        project_kernel,
        out_shape=(
            jax.ShapeDtypeStruct((Y, count, 384), jnp.bfloat16),
            jax.ShapeDtypeStruct((Y, count, 384), jnp.bfloat16),
            jax.ShapeDtypeStruct((Y, 2, count), jnp.float32),
        ),
        in_specs=[pl.BlockSpec(memory_space=pltpu.SMEM)] + [vmem] * 8,
        out_specs=(vmem, vmem, vmem),
        scratch_shapes=[pltpu.VMEM((Y * count, features), jnp.bfloat16)],
        compiler_params=pltpu.CompilerParams(vmem_limit_bytes=40 * 2**20),
        cost_estimate=pl.CostEstimate(
            flops=2 * Y * count * features * 768, bytes_accessed=features * 1536 + Y * count * features * 2,
            transcendentals=0,
        ),
        name="project",
    )(place, scale, shift, weights, *pieces)


def attend_kernel(
    place_ref, power_ref, gain_ref, w_head_ref, own_ref, near_ref, far_ref,
    own_b_ref, near_b_ref, far_b_ref, out_ref, query0, query1, key, value, root,
):
    y_step, c_step = pl.program_id(0), pl.program_id(1)
    my_y, my_z = place_ref[0], place_ref[1]
    my_c = place_ref[2]
    all_cols = HD * 2 * Y * Z * C

    @pl.when((y_step == 0) & (c_step == 0))
    def _():
        totals = []
        for c in range(C):
            total = None
            for y in range(Y):
                for z in range(Z):
                    term = power_ref[(y * Z + z) * C + c]
                    total = term if total is None else total + term
            totals.append(lax.rsqrt(total / all_cols + 1e-6))
        first = lax.select(jnp.broadcast_to(my_c, (16, 128)) == 0, totals[0], totals[1])
        second = lax.select(jnp.broadcast_to(my_c, (16, 128)) == 0, totals[1], totals[0])
        root[0:16, :] = first
        root[16:32, :] = second
        columns = jnp.transpose(root[...])
        lane = lax.broadcasted_iota(jnp.int32, (128, 32), 1)
        head = lax.broadcasted_iota(jnp.int32, (1, 128), 1) < HD
        gain_q = gain_ref[0:1, :] * (HD ** (-0.5) * math.log2(math.e))
        gain_k = gain_ref[1:2, :]
        stacks = ((own_ref, near_ref, far_ref), (own_b_ref, near_b_ref, far_b_ref))
        for slot_c in range(C):
            for slot_y, offset in enumerate(OFFSETS):
                target = lax.rem(my_y + (offset + Y), Y)
                for slot_z in range(Z):
                    z_at = my_z if slot_z == 0 else 1 - my_z
                    at = target * Z + z_at + slot_c * 16
                    scale_q = jnp.sum(jnp.where(lane == at, columns, 0.0), axis=1, keepdims=True)
                    scale_k = jnp.sum(jnp.where(lane == at + 8, columns, 0.0), axis=1, keepdims=True)
                    base = ((slot_c * Y + slot_y) * Z + slot_z) * 128
                    if slot_z == 0:
                        parts = ((stacks[slot_c][0], 0, 128),)
                    else:
                        parts = tuple(
                            (ref, a, b) for ref, (a, b) in zip(stacks[slot_c][1:], CHUNKS)
                        )
                    for ref, a, b in parts:
                        span = slice(base + a, base + b)
                        query = ref[slot_y, :, 0:128].astype(jnp.float32) * scale_q[a:b] * gain_q
                        query0[span, :] = jnp.where(head, query, 0.0).astype(jnp.bfloat16)
                        query1[span, :] = jnp.where(head, 0.0, query).astype(jnp.bfloat16)
                        keys = ref[slot_y, :, 128:256].astype(jnp.float32) * scale_k[a:b] * gain_k
                        key[span, :] = keys.astype(jnp.bfloat16)
                        value[span, 0:128] = ref[slot_y, :, 256:384]
        value[:, 128:256] = jnp.ones((value.shape[0], 128), jnp.bfloat16)

    start = pl.multiple_of((c_step * Y + y_step) * 256, 256)
    outs = []
    for queries in (query0, query1):
        scores = lax.dot_general(
            queries[pl.ds(start, 256), :], key[...], (((1,), (1,)), ((), ())),
            preferred_element_type=jnp.float32,
        )
        highest = jnp.max(scores, axis=-1, keepdims=True)
        raised = jnp.exp2(scores - highest).astype(jnp.bfloat16)
        both = jnp.dot(raised, value[...], preferred_element_type=jnp.float32)
        outs.append(both[:, :128] / both[:, 128:])
    head = lax.broadcasted_iota(jnp.int32, (1, 128), 1) < HD
    attended = jnp.where(head, outs[0], outs[1]).astype(jnp.bfloat16)
    partial = jnp.dot(attended, w_head_ref[...], preferred_element_type=jnp.float32)
    partial = partial.astype(jnp.bfloat16)
    out_ref[0, my_z, 0] = partial[:128]
    out_ref[0, 1 - my_z, 0] = partial[128:]


def attend(place, powers, gains, w_head, mine, theirs):
    tokens = Y * Z * C * 128
    const = lambda rank: (lambda y, c, place: (0,) * rank)
    stack = [pl.BlockSpec(a.shape, const(3)) for a in (*mine, *theirs)]
    y_of = lambda y, place: lax.rem(
        place[0] + jnp.where(y == 0, 0, jnp.where(y == 1, Y - 1, jnp.where(y == 2, 1, 2))), Y
    )
    return pl.pallas_call(
        attend_kernel,
        out_shape=jax.ShapeDtypeStruct((Y, Z, C, 128, 64), jnp.bfloat16),
        grid_spec=pltpu.PrefetchScalarGridSpec(
            num_scalar_prefetch=1,
            grid=(Y, C),
            in_specs=[
                pl.BlockSpec(powers.shape, const(3)),
                pl.BlockSpec(gains.shape, const(2)),
                pl.BlockSpec((128, 64), lambda y, c, place: (place[3], 0)),
                *stack,
            ],
            out_specs=pl.BlockSpec(
                (1, Z, 1, 128, 64),
                lambda y, c, place: (y_of(y, place), 0, lax.rem(c + place[2], C), 0, 0),
            ),
            scratch_shapes=[
                pltpu.VMEM((tokens, 128), jnp.bfloat16),
                pltpu.VMEM((tokens, 128), jnp.bfloat16),
                pltpu.VMEM((tokens, 128), jnp.bfloat16),
                pltpu.VMEM((tokens, 256), jnp.bfloat16),
                pltpu.VMEM((32, 128), jnp.float32),
            ],
        ),
        compiler_params=pltpu.CompilerParams(vmem_limit_bytes=40 * 2**20),
        cost_estimate=pl.CostEstimate(
            flops=tokens * tokens * 1024, bytes_accessed=2**22, transcendentals=2 * tokens * tokens
        ),
        name="attend",
    )(place, powers, gains, w_head, *mine, *theirs)


def layer_norm(token_rows):
    average = jnp.mean(token_rows, axis=-1, keepdims=True)
    centred = token_rows - average
    spread = jnp.mean(centred * centred, axis=-1, keepdims=True)
    return centred * lax.rsqrt(spread + 1e-06)


def spread_over(value, axis, count, groups=None):
    copies = jnp.broadcast_to(value[None], (count,) + value.shape)
    return lax.all_to_all(copies, axis, 0, 0, axis_index_groups=groups)


def per_device(
    x_start, old_states, hidden, modulation, step_index, sigma_table,
    w_query, w_key, w_value, qk_gain, w_head, w_skip,
):
    seq_rank = lax.axis_index("seq").astype(jnp.int32)
    time_rank = lax.axis_index("tm").astype(jnp.int32)
    my_y, my_z, my_c = seq_rank // (Z * C), (seq_rank // C) % Z, seq_rank % C
    my_x, my_zl = time_rank // ZL, time_rank % ZL
    place = jnp.stack([my_y, my_z, my_c, seq_rank])
    raw = hidden[0]

    far = [lax.ppermute(raw[a:b], "seq", TO_FAR) for a, b in CHUNKS]

    w_mine = jnp.concatenate([w_query, w_key, w_value], axis=1)
    w_theirs = lax.ppermute(w_mine, "seq", TO_CORE)
    weights = jnp.concatenate(
        [w[:, i * 128 : (i + 1) * 128] for i in range(3) for w in (w_mine, w_theirs)], axis=1
    )
    following = jnp.concatenate([step_index[1:], step_index[-1:] + 1])
    step_now = lax.dynamic_index_in_dim(step_index, time_rank, 0, False)
    step_next = lax.dynamic_index_in_dim(following, time_rank, 0, False)
    delta = lax.dynamic_index_in_dim(sigma_table, step_next, 0, False) - (
        lax.dynamic_index_in_dim(sigma_table, step_now, 0, False)
    )
    mod_now = lax.dynamic_index_in_dim(modulation, step_now, 0, False)
    scale, shift = mod_now[0:1], mod_now[1:2]
    own_normed = (layer_norm(raw.astype(jnp.float32)) * (1.0 + scale) + shift).astype(jnp.bfloat16)
    skip = jnp.dot(own_normed, w_skip, preferred_element_type=jnp.float32)

    mine, theirs, powers = [], [], []
    for rows in (raw, *far):
        kept, given, power = project(place, scale, shift, weights, along_y(rows))
        mine.append(kept)
        theirs.append(lax.ppermute(given, "seq", TO_CORE))
        powers.append(power)
    power_own = powers[0]
    power_far = jnp.concatenate(powers[1:], axis=2)
    low = jnp.where(my_z == 0, power_own, power_far)
    high = jnp.where(my_z == 0, power_far, power_own)
    table = jnp.stack([low, high], axis=1).transpose(2, 0, 1, 3).reshape(2 * Y * Z, 128)
    powers = spread_over(table, "seq", Y * Z * C)

    partial = attend(place, powers, qk_gain, w_head, mine, theirs)
    partial = lax.all_to_all(partial.reshape(Y * Z * C, 128, 64), "seq", 0, 0)
    drift = jnp.sum(partial.astype(jnp.float32), axis=0) + skip

    increment = delta * drift
    z_groups = [[x * ZL + z for z in range(ZL)] for x in range(4)]
    x_groups = [[x * ZL + z for x in range(4)] for z in range(ZL)]
    line = spread_over(increment.astype(jnp.bfloat16), "tm", ZL, z_groups).astype(jnp.float32)
    total = jnp.sum(line, axis=0)
    before = (jnp.arange(ZL) < my_zl)[:, None, None]
    earlier = jnp.sum(jnp.where(before, line, 0.0), axis=0)
    totals = spread_over(total, "tm", 4, x_groups)
    before = (jnp.arange(4) < my_x)[:, None, None]
    earlier = earlier + jnp.sum(jnp.where(before, totals, 0.0), axis=0)
    new_state = x_start + (earlier + increment)
    change = new_state - old_states[0]
    square = jnp.sum(change * change)
    squares = spread_over(jnp.broadcast_to(square, (1, 128)), "seq", Y * Z * C)
    error = (jnp.sum(squares[:, 0, 0]) / (Y * Z * C * change.size)).reshape(1)
    return (drift[None], new_state[None], error)


def solution(mesh):
    return jax.shard_map(
        per_device,
        mesh=mesh,
        in_specs=(
            P("seq", None),
            P("tm", "seq", None),
            P("tm", "seq", None),
            P(),
            P(),
            P(),
            P(None, "seq"),
            P(None, "seq"),
            P(None, "seq"),
            P(None, "seq"),
            P(),
            P(),
        ),
        out_specs=(P("tm", "seq", None), P("tm", "seq", None), P("tm")),
        check_vma=False,
    )
```

time: 620 us -> 267 us (0.43)
  blocking collectives: 306 us -> 22 us
  waiting for transfers between devices: 222 us -> 57.4 us
  starting transfers between devices: 16.6 us -> 120 us
  Pallas kernels: 0 us -> 32.6 us
  matrix products: 20.9 us -> 1.22 us
  between operations: 18.1 us -> 8.86 us
  loops' own time: 8.42 us -> 0 us
  other arithmetic: 14.3 us -> 7.47 us
    all_gather x1 -> x0, waiting for transfers between devices: 207 us -> none  [per_device(): lax.all_gather(own_normed, 'seq', axis=0, tiled=True)]
    psum x2 -> x0, blocking collectives: 186 us -> none  [the longest x1 110 us: per_device(): lax.psum((jnp.sum(query * query, axis=1), jnp.sum(key_proj * key_proj, ax...]
    all_gather x1 -> x0, blocking collectives: 119 us -> none  [entering(): gathered = lax.all_gather(shard.astype(jnp.bfloat16), axis)]
    ppermute x0 -> x18, starting transfers between devices: none -> 65.8 us  [the longest x2 14 us: per_device(): far = [lax.ppermute(raw[a:b], 'seq', TO_FAR) for a, b in CHUNKS]]
    all_to_all x1 -> x4, starting transfers between devices: 16.6 us -> 54.6 us  [the longest x3 46.4 us: spread_over(): return lax.all_to_all(copies, axis, 0, 0, axis_index_groups=groups)]
    pallas_call x0 -> x4, Pallas kernels: none -> 32.6 us  [the longest x1 18.5 us: attend(): pl.pallas_call(attend_kernel, out_shape=jax.ShapeDtypeStruct((Y, Z, C, 12...]
    ppermute x0 -> x18, waiting for transfers between devices: none -> 25.8 us  [the longest x2 25.7 us: per_device(): far = [lax.ppermute(raw[a:b], 'seq', TO_FAR) for a, b in CHUNKS]]
    all_to_all x0 -> x1, blocking collectives: none -> 22 us  [spread_over(): return lax.all_to_all(copies, axis, 0, 0, axis_index_groups=groups)]
  transfers between devices with their start and end apart: 2 -> 22, of which waited for: 2 -> 6; matrix products, arithmetic and copies ran while one was open for 0% -> 4% of each run, Pallas kernels for 0% -> 4%
where the time goes in v1:
time: 267 us; the launch traced here: 266 us
  starting transfers between devices  120 us (45%)
  waiting for transfers between devices  57.4 us (21%)
  Pallas kernels  32.6 us (12%)
  blocking collectives  22 us (8%)
  local copies, waits for them, and re-layouts  16 us (6%)
  between operations  8.86 us (3%)
  other arithmetic  7.47 us (3%)
    all_to_all x3, starting transfers between devices, spread_over(): return lax.all_to_all(copies, axis, 0, 0, axis_index_groups=groups)  46.4 us
    ppermute x2, waiting for transfers between devices, per_device(): far = [lax.ppermute(raw[a:b], 'seq', TO_FAR) for a, b in CHUNKS]  25.7 us
    all_to_all x1, blocking collectives, spread_over(): return lax.all_to_all(copies, axis, 0, 0, axis_index_groups=groups)  22 us
    all_to_all x3, waiting for transfers between devices, spread_over(): return lax.all_to_all(copies, axis, 0, 0, axis_index_groups=groups)  21.5 us
    pallas_call x1, Pallas kernels, attend(): pl.pallas_call(attend_kernel, out_shape=jax.ShapeDtypeStruct((Y, Z, C, 12...  18.5 us
    pallas_call x3, Pallas kernels, project(): pl.pallas_call(project_kernel, out_shape=(jax.ShapeDtypeStruct((Y, count,...  14.1 us
    ppermute x2, starting transfers between devices, per_device(): far = [lax.ppermute(raw[a:b], 'seq', TO_FAR) for a, b in CHUNKS]  14 us
    ppermute x3, starting transfers between devices, along_y(): lax.ppermute(above[half:], 'seq', TO_DOWN)  13.7 us
  transfers between devices with their start and end apart: 22, of which 6 were waited for; matrix products, arithmetic and copies ran while one was open for 4% of the time, Pallas kernels for 4%

profile of v1, /device:TPU:1, one launch (start us, length us, event | category | flops | bytes accessed | tf_op | source)
XLA Modules:
  0.0 265.9 jit_solution(13981390927113595650)
XLA Ops:
  3.8 8.8 %collective-permute-start = (bf16[2560,384]{1,0:T(8,128)(2,1)}, bf16[2560,384]{1,0:T(8,128)(2,1)}, u32[]{:S(2)}, u32[]{:S(2)}) collective-permute-start(bf16[2560,384]{1,0:T(8,128)(2,1)} %pad_maximum_fusion), channel_id=1, source_target_pairs={{0,1},{1,0},{2,3},{3,2},{4,5},{5,4},{6,7},{7,6},{8,9},{9,8},{10,11... | collective-permute-start | bytes 5898248 | tf_op jit(solution)/shard_map/ppermute | solution.py:243
  14.5 4.6 %collective-permute-start.2 = (bf16[128,2560]{1,0:T(8,128)(2,1)S(1)}, bf16[128,2560]{1,0:T(8,128)(2,1)S(1)}, u32[]{:S(2)}, u32[]{:S(2)}) collective-permute-start(bf16[128,2560]{1,0:T(8,128)(2,1)S(1)} %bitcast.43), channel_id=1, source_target_pairs={{0,12},{1,13},{2,14},{3,15},{4,0},{5,1},{6,2},{7,3},{8,4},{9,5},{1... | collective-permute-start | bytes 1966088 | tf_op jit(solution)/shard_map/ppermute | solution.py:36
  19.9 10.1 %collective-permute-start.10 = (bf16[64,2560]{1,0:T(8,128)(2,1)}, bf16[64,2560]{1,0:T(8,128)(2,1)S(1)}, u32[]{:S(2)}, u32[]{:S(2)}) collective-permute-start(bf16[64,2560]{1,0:T(8,128)(2,1)} %get-tuple-element.30), channel_id=1, source_target_pairs={{0,2},{1,3},{2,0},{3,1},{4,6},{5,7},{6,4},{7,5},{8,10},{9,11},{10,... | collective-permute-start | bytes 983048 | tf_op jit(solution)/shard_map/ppermute | solution.py:240
  30.0 3.9 %collective-permute-start.5 = (bf16[64,2560]{1,0:T(8,128)(2,1)S(1)}, bf16[64,2560]{1,0:T(8,128)(2,1)S(1)}, u32[]{:S(2)}, u32[]{:S(2)}) collective-permute-start(bf16[64,2560]{1,0:T(8,128)(2,1)S(1)} %get-tuple-element.29), channel_id=1, source_target_pairs={{0,2},{1,3},{2,0},{3,1},{4,6},{5,7},{6,4},{7,5},{8,10},{9,11},{10,... | collective-permute-start | bytes 983048 | tf_op jit(solution)/shard_map/ppermute | solution.py:240
  38.0 7.8 %collective-permute-done.10.own_ref = bf16[64,2560]{1,0:T(8,128)(2,1)S(1)} collective-permute-done((bf16[64,2560]{1,0:T(8,128)(2,1)}, bf16[64,2560]{1,0:T(8,128)(2,1)S(1)}, u32[]{:S(2)}, u32[]{:S(2)}) %collective-permute-start.10) | collective-permute-done | bytes 327712 | tf_op jit(solution)/shard_map/ppermute | solution.py:240
  47.7 17.9 %collective-permute-done.5.own_ref = bf16[64,2560]{1,0:T(8,128)(2,1)S(1)} collective-permute-done((bf16[64,2560]{1,0:T(8,128)(2,1)S(1)}, bf16[64,2560]{1,0:T(8,128)(2,1)S(1)}, u32[]{:S(2)}, u32[]{:S(2)}) %collective-permute-start.5) | collective-permute-done | bytes 327712 | tf_op jit(solution)/shard_map/ppermute | solution.py:240
  67.6 3.4 %collective-permute-start.6 = (bf16[64,2560]{1,0:T(8,128)(2,1)S(1)}, bf16[64,2560]{1,0:T(8,128)(2,1)S(1)}, u32[]{:S(2)}, u32[]{:S(2)}) collective-permute-start(bf16[64,2560]{1,0:T(8,128)(2,1)S(1)} %collective-permute-done.5.own_ref), channel_id=1, source_target_pairs={{0,4},{1,5},{2,6},{3,7},{4,8},{5,9},{6,10},{7,11},{8,12},{9,13},{1... | collective-permute-start | bytes 983048 | tf_op jit(solution)/shard_map/ppermute | solution.py:35
  71.0 3.1 %collective-permute-start.7 = (bf16[64,2560]{1,0:T(8,128)(2,1)S(1)}, bf16[64,2560]{1,0:T(8,128)(2,1)S(1)}, u32[]{:S(2)}, u32[]{:S(2)}) collective-permute-start(bf16[64,2560]{1,0:T(8,128)(2,1)S(1)} %collective-permute-done.5.own_ref), channel_id=1, source_target_pairs={{0,12},{1,13},{2,14},{3,15},{4,0},{5,1},{6,2},{7,3},{8,4},{9,5},{1... | collective-permute-start | bytes 983048 | tf_op jit(solution)/shard_map/ppermute | solution.py:36
  77.6 4.3 %collective-permute-start.4 = (bf16[64,2560]{1,0:T(8,128)(2,1)S(1)}, bf16[64,2560]{1,0:T(8,128)(2,1)S(1)}, u32[]{:S(2)}, u32[]{:S(2)}) collective-permute-start(bf16[64,2560]{1,0:T(8,128)(2,1)S(1)} %slice.84), channel_id=1, source_target_pairs={{0,12},{1,13},{2,14},{3,15},{4,0},{5,1},{6,2},{7,3},{8,4},{9,5},{1... | collective-permute-start | bytes 983048 | tf_op jit(solution)/shard_map/ppermute | solution.py:39
  83.9 4.6 %collective-permute-start.14 = (bf16[32,2560]{1,0:T(8,128)(2,1)S(1)}, bf16[32,2560]{1,0:T(8,128)(2,1)S(1)}, u32[]{:S(2)}, u32[]{:S(2)}) collective-permute-start(bf16[32,2560]{1,0:T(8,128)(2,1)S(1)} %slice.88), channel_id=1, source_target_pairs={{0,12},{1,13},{2,14},{3,15},{4,0},{5,1},{6,2},{7,3},{8,4},{9,5},{1... | collective-permute-start | bytes 491528 | tf_op jit(solution)/shard_map/ppermute | solution.py:39
  94.6 4.8 %collective-permute-start.9 = (bf16[32,2560]{1,0:T(8,128)(2,1)S(1)}, bf16[32,2560]{1,0:T(8,128)(2,1)S(1)}, u32[]{:S(2)}, u32[]{:S(2)}) collective-permute-start(bf16[32,2560]{1,0:T(8,128)(2,1)S(1)} %slice.86), channel_id=1, source_target_pairs={{0,12},{1,13},{2,14},{3,15},{4,0},{5,1},{6,2},{7,3},{8,4},{9,5},{1... | collective-permute-start | bytes 491528 | tf_op jit(solution)/shard_map/ppermute | solution.py:39
  99.4 3.5 %project.5 = (bf16[4,64,384]{2,1,0:T(8,128)(2,1)S(1)}, bf16[4,64,384]{2,1,0:T(8,128)(2,1)S(1)}, f32[4,2,64]{2,1,0:T(2,128)S(1)}) custom-call(s32[4]{0:T(128)S(1)} %pad_add_fusion.place_ref, f32[1,2560]{1,0:T(1,128)S(1)} %get-tuple-element.27.scale_ref, f32[1,2560]{1,0:T(1,128)S(1)} %get-tuple-element.28.shift_ref, ...), custom_call_target="tpu_custom_call" | custom-call | flops 1006632960 | bytes 5242880 | tf_op jit(solution)/shard_map/project/pallas_call | solution.py:86
  103.5 7.1 %project.3 = (bf16[4,128,384]{2,1,0:T(8,128)(2,1)S(1)}, bf16[4,128,384]{2,1,0:T(8,128)(2,1)S(1)}, f32[4,2,128]{2,1,0:T(2,128)S(1)}) custom-call(s32[4]{0:T(128)S(1)} %pad_add_fusion.place_ref, f32[1,2560]{1,0:T(1,128)S(1)} %get-tuple-element.27.scale_ref, f32[1,2560]{1,0:T(1,128)S(1)} %get-tuple-element.28.shift_ref, ...), custom_call_target="tpu_custom_call" | custom-call | flops 2013265920 | bytes 6553600 | tf_op jit(solution)/shard_map/project/pallas_call | solution.py:86
  110.7 3.5 %project.4 = (bf16[4,64,384]{2,1,0:T(8,128)(2,1)S(1)}, bf16[4,64,384]{2,1,0:T(8,128)(2,1)S(1)}, f32[4,2,64]{2,1,0:T(2,128)S(1)}) custom-call(s32[4]{0:T(128)S(1)} %pad_add_fusion.place_ref, f32[1,2560]{1,0:T(1,128)S(1)} %get-tuple-element.27.scale_ref, f32[1,2560]{1,0:T(1,128)S(1)} %get-tuple-element.28.shift_ref, ...), custom_call_target="tpu_custom_call" | custom-call | flops 1006632960 | bytes 5242880 | tf_op jit(solution)/shard_map/project/pallas_call | solution.py:86
  115.0 15.7 %all-to-all-start = ((f32[16,16,128]{2,1,0:T(8,128)}), f32[16,16,128]{2,1,0:T(8,128)S(1)}, u32[]{:S(2)}, u32[]{:S(2)}) async-start(f32[16,16,128]{2,1,0:T(8,128)} %broadcast_in_dim.54), calls=%async_computation | async-start | bytes 262144 | tf_op jit(solution)/shard_map/all_to_all | solution.py:226
  139.1 6.3 %all-to-all-done.power_ref = f32[16,16,128]{2,1,0:T(8,128)S(1)} async-done(((f32[16,16,128]{2,1,0:T(8,128)}), f32[16,16,128]{2,1,0:T(8,128)S(1)}, u32[]{:S(2)}, u32[]{:S(2)}) %all-to-all-start) | async-done | bytes 131104 | tf_op jit(solution)/shard_map/all_to_all | solution.py:226
  147.4 18.5 %attend.1 = bf16[4,2,2,128,64]{4,3,2,1,0:T(8,128)(2,1)S(1)} custom-call(s32[4]{0:T(128)S(1)} %pad_add_fusion.place_ref, f32[16,16,128]{2,1,0:T(8,128)S(1)} %all-to-all-done.power_ref, f32[2,128]{1,0:T(2,128)S(1)} %copy-done.6, bf16[2048,64]{1,0:T(8,128)(2,1)S(1)} %copy.31.w_head_ref, bf16[4,128,384]{2,1,0:T(8,128)(2,1)S(1)} %copy-done.8, ...), custom_call_target="tpu_custom_call" | custom-call | flops 4294967296 | bytes 4194304 | tf_op jit(solution)/shard_map/attend/pallas_call | solution.py:185
  166.9 8.2 %all-to-all-start.1 = ((bf16[16,128,64]{1,2,0:T(8,128)(2,1)}), bf16[16,128,64]{1,2,0:T(8,128)(2,1)S(1)}, u32[]{:S(2)}, u32[]{:S(2)}) async-start(bf16[16,128,64]{1,2,0:T(8,128)(2,1)} %copy.32), calls=%async_computation.1 | async-start | bytes 524288 | tf_op jit(solution)/shard_map/all_to_all | solution.py:272
  180.8 10.2 %all-to-all-done.1 = bf16[16,128,64]{1,2,0:T(8,128)(2,1)S(1)} async-done(((bf16[16,128,64]{1,2,0:T(8,128)(2,1)}), bf16[16,128,64]{1,2,0:T(8,128)(2,1)S(1)}, u32[]{:S(2)}, u32[]{:S(2)}) %all-to-all-start.1) | async-done | bytes 262176 | tf_op jit(solution)/shard_map/all_to_all | solution.py:272
  192.9 26.7 %all-to-all-start.2 = ((bf16[8,128,64]{1,2,0:T(8,128)(2,1)}), bf16[8,128,64]{1,2,0:T(8,128)(2,1)S(1)}, u32[]{:S(2)}, u32[]{:S(2)}) async-start(bf16[8,128,64]{1,2,0:T(8,128)(2,1)} %broadcast_in_dim.57), calls=%async_computation.2 | async-start | bytes 262144 | tf_op jit(solution)/shard_map/all_to_all | solution.py:226
  219.6 10.3 %all-to-all-done.2 = bf16[8,128,64]{1,2,0:T(8,128)(2,1)S(1)} async-done(((bf16[8,128,64]{1,2,0:T(8,128)(2,1)}), bf16[8,128,64]{1,2,0:T(8,128)(2,1)S(1)}, u32[]{:S(2)}, u32[]{:S(2)}) %all-to-all-start.2) | async-done | bytes 131104 | tf_op jit(solution)/shard_map/all_to_all | solution.py:226
  230.6 4.0 %all-to-all-start.3 = ((f32[4,128,64]{1,2,0:T(8,128)}), f32[4,128,64]{1,2,0:T(8,128)S(1)}, u32[]{:S(2)}, u32[]{:S(2)}) async-start(f32[4,128,64]{1,2,0:T(8,128)} %broadcast_in_dim.60), calls=%async_computation.3 | async-start | bytes 262144 | tf_op jit(solution)/shard_map/all_to_all | solution.py:226
  234.6 4.8 %all-to-all-done.3 = f32[4,128,64]{1,2,0:T(8,128)S(1)} async-done(((f32[4,128,64]{1,2,0:T(8,128)}), f32[4,128,64]{1,2,0:T(8,128)S(1)}, u32[]{:S(2)}, u32[]{:S(2)}) %all-to-all-start.3) | async-done | bytes 131104 | tf_op jit(solution)/shard_map/all_to_all | solution.py:226
  241.5 22.0 %all_to_all.25 = f32[16,1,128]{2,1,0:T(1,128)S(1)} all-to-all(f32[16,1,128]{2,1,0:T(1,128)S(1)} %broadcast_in_dim_broadcast_in_dim_broadcast_in_dim.3), channel_id=1, replica_groups=mesh['tm'=32,'seq'=16] {'seq'}, dimensions={0} | all-to-all | bytes 16384 | tf_op jit(solution)/shard_map/all_to_all | solution.py:226
  (99 shorter events, 43.0 us)
Async XLA Ops:
  0.6 190.3 %copy-start = (bf16[2560,64]{0,1:T(8,128)(2,1)S(1)}, bf16[2560,64]{0,1:T(8,128)(2,1)}, u32[]{:S(2)}) copy-start(bf16[2560,64]{0,1:T(8,128)(2,1)} %param.23) | copy-start | bytes 983044
  3.8 84.8 %collective-permute-start = (bf16[2560,384]{1,0:T(8,128)(2,1)}, bf16[2560,384]{1,0:T(8,128)(2,1)}, u32[]{:S(2)}, u32[]{:S(2)}) collective-permute-start(bf16[2560,384]{1,0:T(8,128)(2,1)} %pad_maximum_fusion), channel_id=1, source_target_pairs={{0,1},{1,0},{2,3},{3,2},{4,5},{5,4},{6,7},{7,6},{8,9},{9,8},{10,11... | collective-permute-start | bytes 5898248 | tf_op jit(solution)/shard_map/ppermute | solution.py:243
  12.6 55.0 %collective-permute-start.1 = (bf16[128,2560]{1,0:T(8,128)(2,1)S(1)}, bf16[128,2560]{1,0:T(8,128)(2,1)S(1)}, u32[]{:S(2)}, u32[]{:S(2)}) collective-permute-start(bf16[128,2560]{1,0:T(8,128)(2,1)S(1)} %bitcast.42), channel_id=1, source_target_pairs={{0,4},{1,5},{2,6},{3,7},{4,8},{5,9},{6,10},{7,11},{8,12},{9,13},{1... | collective-permute-start | bytes 1966088 | tf_op jit(solution)/shard_map/ppermute | solution.py:35
  14.5 56.5 %collective-permute-start.2 = (bf16[128,2560]{1,0:T(8,128)(2,1)S(1)}, bf16[128,2560]{1,0:T(8,128)(2,1)S(1)}, u32[]{:S(2)}, u32[]{:S(2)}) collective-permute-start(bf16[128,2560]{1,0:T(8,128)(2,1)S(1)} %bitcast.43), channel_id=1, source_target_pairs={{0,12},{1,13},{2,14},{3,15},{4,0},{5,1},{6,2},{7,3},{8,4},{9,5},{1... | collective-permute-start | bytes 1966088 | tf_op jit(solution)/shard_map/ppermute | solution.py:36
  19.9 26.0 %collective-permute-start.10 = (bf16[64,2560]{1,0:T(8,128)(2,1)}, bf16[64,2560]{1,0:T(8,128)(2,1)S(1)}, u32[]{:S(2)}, u32[]{:S(2)}) collective-permute-start(bf16[64,2560]{1,0:T(8,128)(2,1)} %get-tuple-element.30), channel_id=1, source_target_pairs={{0,2},{1,3},{2,0},{3,1},{4,6},{5,7},{6,4},{7,5},{8,10},{9,11},{10,... | collective-permute-start | bytes 983048 | tf_op jit(solution)/shard_map/ppermute | solution.py:240
  30.0 35.7 %collective-permute-start.5 = (bf16[64,2560]{1,0:T(8,128)(2,1)S(1)}, bf16[64,2560]{1,0:T(8,128)(2,1)S(1)}, u32[]{:S(2)}, u32[]{:S(2)}) collective-permute-start(bf16[64,2560]{1,0:T(8,128)(2,1)S(1)} %get-tuple-element.29), channel_id=1, source_target_pairs={{0,2},{1,3},{2,0},{3,1},{4,6},{5,7},{6,4},{7,5},{8,10},{9,11},{10,... | collective-permute-start | bytes 983048 | tf_op jit(solution)/shard_map/ppermute | solution.py:240
  45.8 29.6 %collective-permute-start.11 = (bf16[64,2560]{1,0:T(8,128)(2,1)S(1)}, bf16[64,2560]{1,0:T(8,128)(2,1)S(1)}, u32[]{:S(2)}, u32[]{:S(2)}) collective-permute-start(bf16[64,2560]{1,0:T(8,128)(2,1)S(1)} %collective-permute-done.10.own_ref), channel_id=1, source_target_pairs={{0,4},{1,5},{2,6},{3,7},{4,8},{5,9},{6,10},{7,11},{8,12},{9,13},{1... | collective-permute-start | bytes 983048 | tf_op jit(solution)/shard_map/ppermute | solution.py:35
  65.7 11.9 %collective-permute-start.12 = (bf16[64,2560]{1,0:T(8,128)(2,1)S(1)}, bf16[64,2560]{1,0:T(8,128)(2,1)S(1)}, u32[]{:S(2)}, u32[]{:S(2)}) collective-permute-start(bf16[64,2560]{1,0:T(8,128)(2,1)S(1)} %collective-permute-done.10.own_ref), channel_id=1, source_target_pairs={{0,12},{1,13},{2,14},{3,15},{4,0},{5,1},{6,2},{7,3},{8,4},{9,5},{1... | collective-permute-start | bytes 983048 | tf_op jit(solution)/shard_map/ppermute | solution.py:36
  67.6 14.4 %collective-permute-start.6 = (bf16[64,2560]{1,0:T(8,128)(2,1)S(1)}, bf16[64,2560]{1,0:T(8,128)(2,1)S(1)}, u32[]{:S(2)}, u32[]{:S(2)}) collective-permute-start(bf16[64,2560]{1,0:T(8,128)(2,1)S(1)} %collective-permute-done.5.own_ref), channel_id=1, source_target_pairs={{0,4},{1,5},{2,6},{3,7},{4,8},{5,9},{6,10},{7,11},{8,12},{9,13},{1... | collective-permute-start | bytes 983048 | tf_op jit(solution)/shard_map/ppermute | solution.py:35
  71.0 12.9 %collective-permute-start.7 = (bf16[64,2560]{1,0:T(8,128)(2,1)S(1)}, bf16[64,2560]{1,0:T(8,128)(2,1)S(1)}, u32[]{:S(2)}, u32[]{:S(2)}) collective-permute-start(bf16[64,2560]{1,0:T(8,128)(2,1)S(1)} %collective-permute-done.5.own_ref), channel_id=1, source_target_pairs={{0,12},{1,13},{2,14},{3,15},{4,0},{5,1},{6,2},{7,3},{8,4},{9,5},{1... | collective-permute-start | bytes 983048 | tf_op jit(solution)/shard_map/ppermute | solution.py:36
  75.4 28.1 %collective-permute-start.3 = (bf16[64,2560]{1,0:T(8,128)(2,1)S(1)}, bf16[64,2560]{1,0:T(8,128)(2,1)S(1)}, u32[]{:S(2)}, u32[]{:S(2)}) collective-permute-start(bf16[64,2560]{1,0:T(8,128)(2,1)S(1)} %slice.83), channel_id=1, source_target_pairs={{0,4},{1,5},{2,6},{3,7},{4,8},{5,9},{6,10},{7,11},{8,12},{9,13},{1... | collective-permute-start | bytes 983048 | tf_op jit(solution)/shard_map/ppermute | solution.py:38
  77.6 25.9 %collective-permute-start.4 = (bf16[64,2560]{1,0:T(8,128)(2,1)S(1)}, bf16[64,2560]{1,0:T(8,128)(2,1)S(1)}, u32[]{:S(2)}, u32[]{:S(2)}) collective-permute-start(bf16[64,2560]{1,0:T(8,128)(2,1)S(1)} %slice.84), channel_id=1, source_target_pairs={{0,12},{1,13},{2,14},{3,15},{4,0},{5,1},{6,2},{7,3},{8,4},{9,5},{1... | collective-permute-start | bytes 983048 | tf_op jit(solution)/shard_map/ppermute | solution.py:39
  82.0 12.6 %collective-permute-start.13 = (bf16[32,2560]{1,0:T(8,128)(2,1)S(1)}, bf16[32,2560]{1,0:T(8,128)(2,1)S(1)}, u32[]{:S(2)}, u32[]{:S(2)}) collective-permute-start(bf16[32,2560]{1,0:T(8,128)(2,1)S(1)} %slice.87), channel_id=1, source_target_pairs={{0,4},{1,5},{2,6},{3,7},{4,8},{5,9},{6,10},{7,11},{8,12},{9,13},{1... | collective-permute-start | bytes 491528 | tf_op jit(solution)/shard_map/ppermute | solution.py:38
  83.9 15.4 %collective-permute-start.14 = (bf16[32,2560]{1,0:T(8,128)(2,1)S(1)}, bf16[32,2560]{1,0:T(8,128)(2,1)S(1)}, u32[]{:S(2)}, u32[]{:S(2)}) collective-permute-start(bf16[32,2560]{1,0:T(8,128)(2,1)S(1)} %slice.88), channel_id=1, source_target_pairs={{0,12},{1,13},{2,14},{3,15},{4,0},{5,1},{6,2},{7,3},{8,4},{9,5},{1... | collective-permute-start | bytes 491528 | tf_op jit(solution)/shard_map/ppermute | solution.py:39
  88.6 22.1 %collective-permute-start.8 = (bf16[32,2560]{1,0:T(8,128)(2,1)S(1)}, bf16[32,2560]{1,0:T(8,128)(2,1)S(1)}, u32[]{:S(2)}, u32[]{:S(2)}) collective-permute-start(bf16[32,2560]{1,0:T(8,128)(2,1)S(1)} %slice.85), channel_id=1, source_target_pairs={{0,4},{1,5},{2,6},{3,7},{4,8},{5,9},{6,10},{7,11},{8,12},{9,13},{1... | collective-permute-start | bytes 491528 | tf_op jit(solution)/shard_map/ppermute | solution.py:38
  94.6 16.1 %collective-permute-start.9 = (bf16[32,2560]{1,0:T(8,128)(2,1)S(1)}, bf16[32,2560]{1,0:T(8,128)(2,1)S(1)}, u32[]{:S(2)}, u32[]{:S(2)}) collective-permute-start(bf16[32,2560]{1,0:T(8,128)(2,1)S(1)} %slice.86), channel_id=1, source_target_pairs={{0,12},{1,13},{2,14},{3,15},{4,0},{5,1},{6,2},{7,3},{8,4},{9,5},{1... | collective-permute-start | bytes 491528 | tf_op jit(solution)/shard_map/ppermute | solution.py:39
  115.0 30.5 %all-to-all-start = ((f32[16,16,128]{2,1,0:T(8,128)}), f32[16,16,128]{2,1,0:T(8,128)S(1)}, u32[]{:S(2)}, u32[]{:S(2)}) async-start(f32[16,16,128]{2,1,0:T(8,128)} %broadcast_in_dim.54), calls=%async_computation | async-start | bytes 262144 | tf_op jit(solution)/shard_map/all_to_all | solution.py:226
  130.6 8.5 %collective-permute-start.15 = (bf16[4,128,384]{2,1,0:T(8,128)(2,1)S(1)}, bf16[4,128,384]{2,1,0:T(8,128)(2,1)S(1)}, u32[]{:S(2)}, u32[]{:S(2)}) collective-permute-start(bf16[4,128,384]{2,1,0:T(8,128)(2,1)S(1)} %get-tuple-element.18), channel_id=1, source_target_pairs={{0,1},{1,0},{2,3},{3,2},{4,5},{5,4},{6,7},{7,6},{8,9},{9,8},{10,11... | collective-permute-start | bytes 1179656 | tf_op jit(solution)/shard_map/ppermute | solution.py:262
  132.7 5.8 %collective-permute-start.16 = (bf16[4,64,384]{2,1,0:T(8,128)(2,1)S(1)}, bf16[4,64,384]{2,1,0:T(8,128)(2,1)S(1)}, u32[]{:S(2)}, u32[]{:S(2)}) collective-permute-start(bf16[4,64,384]{2,1,0:T(8,128)(2,1)S(1)} %get-tuple-element.19), channel_id=1, source_target_pairs={{0,1},{1,0},{2,3},{3,2},{4,5},{5,4},{6,7},{7,6},{8,9},{9,8},{10,11... | collective-permute-start | bytes 589832 | tf_op jit(solution)/shard_map/ppermute | solution.py:262
  135.0 4.2 %collective-permute-start.17 = (bf16[4,64,384]{2,1,0:T(8,128)(2,1)S(1)}, bf16[4,64,384]{2,1,0:T(8,128)(2,1)}, u32[]{:S(2)}, u32[]{:S(2)}) collective-permute-start(bf16[4,64,384]{2,1,0:T(8,128)(2,1)S(1)} %copy-done.3), channel_id=1, source_target_pairs={{0,1},{1,0},{2,3},{3,2},{4,5},{5,4},{6,7},{7,6},{8,9},{9,8},{10,11... | collective-permute-start | bytes 589832 | tf_op jit(solution)/shard_map/ppermute | solution.py:262
  166.0 73.6 %copy-start.11 = (f32[1,128,64]{1,2,0:T(8,128)S(1)}, f32[1,128,64]{1,2,0:T(8,128)}, u32[]{:S(2)}) copy-start(f32[1,128,64]{1,2,0:T(8,128)} %param.13) | copy-start | bytes 98308
  166.9 24.0 %all-to-all-start.1 = ((bf16[16,128,64]{1,2,0:T(8,128)(2,1)}), bf16[16,128,64]{1,2,0:T(8,128)(2,1)S(1)}, u32[]{:S(2)}, u32[]{:S(2)}) async-start(bf16[16,128,64]{1,2,0:T(8,128)(2,1)} %copy.32), calls=%async_computation.1 | async-start | bytes 524288 | tf_op jit(solution)/shard_map/all_to_all | solution.py:272
  192.9 37.0 %all-to-all-start.2 = ((bf16[8,128,64]{1,2,0:T(8,128)(2,1)}), bf16[8,128,64]{1,2,0:T(8,128)(2,1)S(1)}, u32[]{:S(2)}, u32[]{:S(2)}) async-start(bf16[8,128,64]{1,2,0:T(8,128)(2,1)} %broadcast_in_dim.57), calls=%async_computation.2 | async-start | bytes 262144 | tf_op jit(solution)/shard_map/all_to_all | solution.py:226
  230.6 8.9 %all-to-all-start.3 = ((f32[4,128,64]{1,2,0:T(8,128)}), f32[4,128,64]{1,2,0:T(8,128)S(1)}, u32[]{:S(2)}, u32[]{:S(2)}) async-start(f32[4,128,64]{1,2,0:T(8,128)} %broadcast_in_dim.60), calls=%async_computation.3 | async-start | bytes 262144 | tf_op jit(solution)/shard_map/all_to_all | solution.py:226
  (14 other events, 398.7 us)

commit v2 on v1

v2 whole, which is shorter than its diff:
```python
import functools
import math

import jax
import jax.numpy as jnp
from jax import lax
from jax.experimental import pallas as pl
from jax.experimental.pallas import tpu as pltpu
from jax.sharding import PartitionSpec as P

HD = 64
LAT = 64
Y, Z, C = 4, 2, 2
ZL = 8


Z_GROUPS = [
    [(x * ZL + zl) * Y * Z * C + (y * Z + z) * C + c for z in range(Z) for zl in range(ZL)]
    for x in range(4)
    for y in range(Y)
    for c in range(C)
]


def seq_perm(move):
    pairs = []
    for s in range(Y * Z * C):
        y, z, c = s // (Z * C), (s // C) % Z, s % C
        y, z, c = move(y, z, c)
        pairs.append((s, ((y % Y) * Z + z) * C + c))
    return pairs


TO_CORE = seq_perm(lambda y, z, c: (y, z, 1 - c))
Y_GROUPS = [[y * Z * C + r for y in range(Y)] for r in range(Z * C)]
YC_GROUPS = [[(y * Z + z) * C + c for y in range(Y) for c in range(C)] for z in range(Z)]
TO_UP = seq_perm(lambda y, z, c: (y + 1, z, c))
TO_DOWN = seq_perm(lambda y, z, c: (y - 1, z, c))
TO_FAR = seq_perm(lambda y, z, c: (y, 1 - z, c))


def along_y(rows):
    half = rows.shape[0] // 2
    below = lax.ppermute(rows, "seq", TO_UP)
    above = lax.ppermute(rows, "seq", TO_DOWN)
    return (
        rows, below, above,
        lax.ppermute(below[:half], "seq", TO_UP), lax.ppermute(above[half:], "seq", TO_DOWN),
    )


def project_kernel(
    order_ref, scale_ref, shift_ref, w_mine, w_theirs, rows_ref, mine_ref, other_ref, power_ref
):
    rows = rows_ref[...].astype(jnp.float32)
    average = jnp.mean(rows, axis=-1, keepdims=True)
    centred = rows - average
    spread = jnp.mean(centred * centred, axis=-1, keepdims=True)
    normed = centred * lax.rsqrt(spread + 1e-6) * (1.0 + scale_ref[...]) + shift_ref[...]
    normed = normed.astype(jnp.bfloat16)
    mine = jnp.dot(normed, w_mine[...], preferred_element_type=jnp.float32)
    other = jnp.dot(normed, w_theirs[...], preferred_element_type=jnp.float32)
    mine_ref[0] = mine
    other_ref[0] = other
    for part in range(2):
        cols = slice(part * 128, (part + 1) * 128)
        squares = mine[:, cols] * mine[:, cols] + other[:, cols] * other[:, cols]
        power_ref[0, part : part + 1, :] = jnp.sum(jnp.transpose(squares), axis=0, keepdims=True)


def project(order, scale, shift, w_mine, w_theirs, rows):
    features, columns = w_mine.shape
    count = rows.shape[0] // Y
    vmem = pl.BlockSpec(memory_space=pltpu.VMEM)
    stack = pl.BlockSpec((1, count, columns), lambda y, order: (order[y], 0, 0))
    return pl.pallas_call(
        project_kernel,
        out_shape=(
            jax.ShapeDtypeStruct((Y, count, columns), jnp.float32),
            jax.ShapeDtypeStruct((Y, count, columns), jnp.float32),
            jax.ShapeDtypeStruct((Y, 2, count), jnp.float32),
        ),
        grid_spec=pltpu.PrefetchScalarGridSpec(
            num_scalar_prefetch=1,
            grid=(Y,),
            in_specs=[vmem, vmem, vmem, vmem, pl.BlockSpec((count, features), lambda y, order: (y, 0))],
            out_specs=(stack, stack, pl.BlockSpec((1, 2, count), lambda y, order: (order[y], 0, 0))),
        ),
        compiler_params=pltpu.CompilerParams(vmem_limit_bytes=24 * 2**20),
        cost_estimate=pl.CostEstimate(
            flops=2 * Y * count * features * 768,
            bytes_accessed=features * 1536 + Y * count * features * 2,
            transcendentals=0,
        ),
        name="project",
    )(order, scale, shift, w_mine, w_theirs, rows)


def attend_kernel(chunks, place_ref, power_ref, gain_ref, w_head_ref, *refs):
    stacks = (refs[: len(chunks)], refs[len(chunks) : 2 * len(chunks)])
    out_ref, query0, query1, key0, key1, value, root = refs[2 * len(chunks) :]
    c_step = pl.program_id(0)
    my_z, my_c = place_ref[1], place_ref[2]
    all_cols = HD * 2 * Y * Z * C
    head = lax.broadcasted_iota(jnp.int32, (1, 128), 1) < HD

    @pl.when(c_step == 0)
    def _():
        totals = []
        for c in range(C):
            total = None
            for y in range(Y):
                for z in range(Z):
                    term = power_ref[(y * Z + z) * C + c]
                    total = term if total is None else total + term
            totals.append(lax.rsqrt(total / all_cols + 1e-6))
        flip = jnp.broadcast_to(my_c, (16, 128)) == 0
        root[0:16, :] = jnp.where(flip, totals[0], totals[1])
        root[16:32, :] = jnp.where(flip, totals[1], totals[0])
        columns = jnp.transpose(root[...])
        lane = lax.broadcasted_iota(jnp.int32, (128, 32), 1)
        gain_q = gain_ref[0:1, :]
        gain_k = gain_ref[1:2, :]
        for slot_c in range(C):
            for slot_y in range(Y):
                for slot_z in range(Z):
                    z_at = my_z if slot_z == 0 else 1 - my_z
                    at = slot_y * Z + z_at + slot_c * 16
                    scale_q = jnp.sum(jnp.where(lane == at, columns, 0.0), axis=1, keepdims=True)
                    scale_k = jnp.sum(jnp.where(lane == at + 8, columns, 0.0), axis=1, keepdims=True)
                    base = ((slot_c * Y + slot_y) * Z + slot_z) * 128
                    for ref, (kind, a, b) in zip(stacks[slot_c], chunks):
                        if kind != slot_z:
                            continue
                        span = slice(base + a, base + b)
                        unit = (ref[slot_y, :, 0:128] * scale_q[a:b] * gain_q).astype(jnp.bfloat16)
                        query = unit.astype(jnp.float32) * (HD ** (-0.5) * math.log2(math.e))
                        high = query.astype(jnp.bfloat16).astype(jnp.float32)
                        low = pltpu.roll(query - high, HD, 1)
                        query0[span, :] = jnp.where(head, high, low).astype(jnp.bfloat16)
                        query1[span, :] = jnp.where(head, low, high).astype(jnp.bfloat16)
                        keys = ref[slot_y, :, 128:256] * scale_k[a:b] * gain_k
                        turned = pltpu.roll(keys, HD, 1)
                        key0[span, :] = jnp.where(head, keys, turned).astype(jnp.bfloat16)
                        key1[span, :] = jnp.where(head, turned, keys).astype(jnp.bfloat16)
                        value[span, 0:128] = ref[slot_y, :, 256:384].astype(jnp.bfloat16)
        value[:, 128:256] = jnp.ones((value.shape[0], 128), jnp.bfloat16)

    count = Y * Z * 128
    start = pl.multiple_of(c_step * count, count)
    scores = [
        lax.dot_general(
            queries[pl.ds(start, count), :], keys[...], (((1,), (1,)), ((), ())),
            preferred_element_type=jnp.float32,
        )
        for queries, keys in ((query0, key0), (query1, key1))
    ]
    raised = [
        jnp.exp2(part - jnp.max(part, axis=-1, keepdims=True)).astype(jnp.bfloat16)
        for part in scores
    ]
    both = [jnp.dot(part, value[...], preferred_element_type=jnp.float32) for part in raised]
    outs = [part[:, :128] / part[:, 128:] for part in both]
    attended = jnp.where(head, outs[0], outs[1]).astype(jnp.bfloat16)
    partial = lax.dot_general(
        w_head_ref[...], attended, (((0,), (1,)), ((), ())), preferred_element_type=jnp.float32
    ).astype(jnp.bfloat16)
    for y in range(Y):
        at = y * Z * 128
        out_ref[y, 0, my_z] = partial[:, at : at + 128]
        out_ref[y, 0, 1 - my_z] = partial[:, at + 128 : at + 256]


def attend(chunks, place, powers, gains, w_head, mine, theirs):
    tokens = Y * Z * C * 128
    const = lambda rank: (lambda c, place: (0,) * rank)
    stack = [pl.BlockSpec(a.shape, const(3)) for a in (*mine, *theirs)]
    return pl.pallas_call(
        functools.partial(attend_kernel, chunks),
        out_shape=jax.ShapeDtypeStruct((Y, C, Z, 64, 128), jnp.bfloat16),
        grid_spec=pltpu.PrefetchScalarGridSpec(
            num_scalar_prefetch=1,
            grid=(C,),
            in_specs=[
                pl.BlockSpec(powers.shape, const(3)),
                pl.BlockSpec(gains.shape, const(2)),
                pl.BlockSpec((128, LAT), lambda c, place: (place[3], 0)),
                *stack,
            ],
            out_specs=pl.BlockSpec(
                (Y, 1, Z, LAT, 128),
                lambda c, place: (0, lax.rem(c + place[2], C), 0, 0, 0),
            ),
            scratch_shapes=[pltpu.VMEM((tokens, 128), jnp.bfloat16)] * 4
            + [pltpu.VMEM((tokens, 256), jnp.bfloat16), pltpu.VMEM((32, 128), jnp.float32)],
        ),
        compiler_params=pltpu.CompilerParams(vmem_limit_bytes=56 * 2**20),
        cost_estimate=pl.CostEstimate(
            flops=tokens * tokens * 1024, bytes_accessed=2**22, transcendentals=2 * tokens * tokens
        ),
        name="attend",
    )(place, powers, gains, w_head, *mine, *theirs)


def layer_norm(token_rows):
    average = jnp.mean(token_rows, axis=-1, keepdims=True)
    centred = token_rows - average
    spread = jnp.mean(centred * centred, axis=-1, keepdims=True)
    return centred * lax.rsqrt(spread + 1e-06)


def spread_over(value, axis, count, groups=None):
    copies = jnp.broadcast_to(value[None], (count,) + value.shape)
    return lax.all_to_all(copies, axis, 0, 0, axis_index_groups=groups)


def per_device(
    x_start, old_states, hidden, modulation, step_index, sigma_table,
    w_query, w_key, w_value, qk_gain, w_head, w_skip,
):
    seq_rank = lax.axis_index("seq").astype(jnp.int32)
    time_rank = lax.axis_index("tm").astype(jnp.int32)
    my_y, my_z, my_c = seq_rank // (Z * C), (seq_rank // C) % Z, seq_rank % C
    my_x, my_zl = time_rank // ZL, time_rank % ZL
    place = jnp.stack([my_y, my_z, my_c, seq_rank])
    raw = hidden[0]

    far = lax.ppermute(raw, "seq", TO_FAR)
    own = along_y(raw)
    w_parts, _ = lax.optimization_barrier(((w_query, w_key, w_value), own[1:3]))
    w_mine = jnp.concatenate(w_parts, axis=1)
    w_theirs = lax.ppermute(w_mine, "seq", TO_CORE)
    following = jnp.concatenate([step_index[1:], step_index[-1:] + 1])
    step_now = lax.dynamic_index_in_dim(step_index, time_rank, 0, False)
    step_next = lax.dynamic_index_in_dim(following, time_rank, 0, False)
    delta = lax.dynamic_index_in_dim(sigma_table, step_next, 0, False) - (
        lax.dynamic_index_in_dim(sigma_table, step_now, 0, False)
    )
    mod_now = lax.dynamic_index_in_dim(modulation, step_now, 0, False)
    scale, shift = mod_now[0:1], mod_now[1:2]
    own_normed = (layer_norm(raw.astype(jnp.float32)) * (1.0 + scale) + shift).astype(jnp.bfloat16)
    skip = jnp.dot(own_normed, w_skip, preferred_element_type=jnp.float32)

    mine, theirs, powers = [], [], []

    def project_stack(order, rows):
        kept, given, power = project(order, scale, shift, w_mine, w_theirs, rows)
        mine.append(kept)
        theirs.append(lax.ppermute(given, "seq", TO_CORE))
        powers.append(power)

    far, own = lax.optimization_barrier((far, own))
    far = spread_over(far, "seq", Y, Y_GROUPS).reshape(-1, raw.shape[1])
    project_stack(jnp.stack([my_y, my_y + 3, my_y + 1, my_y + 2]) % Y, jnp.concatenate(own))
    project_stack(jnp.arange(Y, dtype=jnp.int32), far)
    power_own, power_far = powers
    low = jnp.where(my_z == 0, power_own, power_far)
    high = jnp.where(my_z == 0, power_far, power_own)
    table = jnp.stack([low, high], axis=1).transpose(2, 0, 1, 3).reshape(2 * Y * Z, 128)
    powers = spread_over(table, "seq", Y * Z * C)

    chunks = ((0, 0, 128), (1, 0, 128))
    partial = attend(chunks, place, powers, qk_gain, w_head, mine, theirs)
    partial = partial.reshape(Y * C, Z, LAT, 128)
    partial = lax.all_to_all(partial, "seq", 0, 0, axis_index_groups=YC_GROUPS)
    partial = jnp.sum(partial.astype(jnp.float32), axis=0)
    here = lax.dynamic_index_in_dim(partial, my_z, 0, False) + skip.T
    owner = (jnp.arange(Z) == my_z)[:, None, None]
    sent = jnp.where(owner, here[None], partial).astype(jnp.bfloat16)
    sent = jnp.broadcast_to(sent[:, None], (Z, ZL, LAT, 128)).reshape(Z * ZL, LAT, 128)
    line = lax.all_to_all(sent, ("tm", "seq"), 0, 0, axis_index_groups=Z_GROUPS)
    line = line.reshape(Z, ZL, LAT, 128).astype(jnp.float32)
    there = lax.dynamic_index_in_dim(line, 1 - my_z, 0, False)
    drift = here + lax.dynamic_index_in_dim(there, my_zl, 0, False)
    increment = delta * drift
    steps = jnp.concatenate([step_index, step_index[-1:] + 1])
    sigmas = jnp.dot(
        (steps[:, None] == jnp.arange(sigma_table.shape[0])).astype(jnp.float32), sigma_table,
        precision=lax.Precision.HIGHEST,
    )
    deltas = lax.dynamic_slice_in_dim(sigmas[1:] - sigmas[:-1], my_x * ZL, ZL, 0)
    line = jnp.sum(line, axis=0) * deltas[:, None, None]
    total = jnp.sum(line, axis=0)
    before = (jnp.arange(ZL) < my_zl)[:, None, None]
    earlier = jnp.sum(jnp.where(before, line, 0.0), axis=0)
    x_groups = [[x * ZL + z for x in range(4)] for z in range(ZL)]
    totals = spread_over(total, "tm", 4, x_groups)
    before = (jnp.arange(4) < my_x)[:, None, None]
    earlier = earlier + jnp.sum(jnp.where(before, totals, 0.0), axis=0)
    new_state = x_start.T + (earlier + increment)
    change = new_state - old_states[0].T
    square = jnp.sum(change * change)
    squares = spread_over(jnp.broadcast_to(square, (1, 128)), "seq", Y * Z * C)
    error = (jnp.sum(squares[:, 0, 0]) / (Y * Z * C * change.size)).reshape(1)
    return (drift.T[None], new_state.T[None], error)


def solution(mesh):
    return jax.shard_map(
        per_device,
        mesh=mesh,
        in_specs=(
            P("seq", None),
            P("tm", "seq", None),
            P("tm", "seq", None),
            P(),
            P(),
            P(),
            P(None, "seq"),
            P(None, "seq"),
            P(None, "seq"),
            P(None, "seq"),
            P(),
            P(),
        ),
        out_specs=(P("tm", "seq", None), P("tm", "seq", None), P("tm")),
        check_vma=False,
    )
```

time: 267 us -> 248 us (0.929)
  waiting for transfers between devices: 57.4 us -> 40.7 us
  starting transfers between devices: 120 us -> 112 us
  blocking collectives: 22 us -> 28.1 us
    all_to_all x1 -> x2, starting transfers between devices: 8.15 us -> 42.1 us  [the longest x1 38.1 us: per_device(): line = lax.all_to_all(sent, ('tm', 'seq'), 0, 0, axis_index_groups=Z_GROUPS)]
    ppermute x5 -> x3, waiting for transfers between devices: 25.8 us -> 1.85 us  [the longest x1 1.85 us: per_device(): far = lax.ppermute(raw, 'seq', TO_FAR)]
    all_to_all x3, starting transfers between devices: 46.4 us -> 25.8 us  [spread_over(): return lax.all_to_all(copies, axis, 0, 0, axis_index_groups=groups)]
    ppermute x3 -> x1, starting transfers between devices: 13.7 us -> 4.7 us  [along_y(): lax.ppermute(above[half:], 'seq', TO_DOWN)]
    ppermute x3 -> x1, starting transfers between devices: 9.61 us -> 3.36 us  [along_y(): above = lax.ppermute(rows, 'seq', TO_DOWN)]
    all_to_all x1, blocking collectives: 22 us -> 28.1 us  [spread_over(): return lax.all_to_all(copies, axis, 0, 0, axis_index_groups=groups)]
    ppermute x5 -> x3, starting transfers between devices: 20.5 us -> 26 us  [the longest x1 15.4 us: per_device(): far = lax.ppermute(raw, 'seq', TO_FAR)]
    ppermute x1, starting transfers between devices: 8.78 us -> 3.9 us  [per_device(): w_theirs = lax.ppermute(w_mine, 'seq', TO_CORE)]
  transfers between devices with their start and end apart: 22 -> 13, of which waited for: 6 -> 6; matrix products, arithmetic and copies ran while one was open for 4% -> 7% of each run, Pallas kernels for 4% -> 7%
where the time goes in v2:
time: 248 us; the launch traced here: 247 us
  starting transfers between devices  112 us (45%)
  waiting for transfers between devices  40.7 us (16%)
  Pallas kernels  32.3 us (13%)
  blocking collectives  28.1 us (11%)
  local copies, waits for them, and re-layouts  17.5 us (7%)
  between operations  8.75 us (4%)
  other arithmetic  6.82 us (3%)
    all_to_all x1, starting transfers between devices, per_device(): line = lax.all_to_all(sent, ('tm', 'seq'), 0, 0, axis_index_groups=Z_GROUPS)  38.1 us
    all_to_all x1, blocking collectives, spread_over(): return lax.all_to_all(copies, axis, 0, 0, axis_index_groups=groups)  28.1 us
    all_to_all x3, starting transfers between devices, spread_over(): return lax.all_to_all(copies, axis, 0, 0, axis_index_groups=groups)  25.8 us
    all_to_all x3, waiting for transfers between devices, spread_over(): return lax.all_to_all(copies, axis, 0, 0, axis_index_groups=groups)  25.1 us
    pallas_call x2, Pallas kernels, project(): pl.pallas_call(project_kernel, out_shape=(jax.ShapeDtypeStruct((Y, count,...  17 us
    ppermute x1, starting transfers between devices, per_device(): far = lax.ppermute(raw, 'seq', TO_FAR)  15.4 us
    pallas_call x1, Pallas kernels, attend(): pl.pallas_call(functools.partial(attend_kernel, chunks), out_shape=jax.Sh...  15.3 us
    ppermute x2, starting transfers between devices, project_stack(): theirs.append(lax.ppermute(given, 'seq', TO_CORE))  10.5 us
  transfers between devices with their start and end apart: 13, of which 6 were waited for; matrix products, arithmetic and copies ran while one was open for 7% of the time, Pallas kernels for 7%

profile of v2, /device:TPU:1, one launch (start us, length us, event | category | flops | bytes accessed | tf_op | source)
XLA Modules:
  0.0 246.9 jit_solution(8126405133003357059)
XLA Ops:
  0.7 4.2 %collective-permute-start = (bf16[128,2560]{1,0:T(8,128)(2,1)}, bf16[128,2560]{1,0:T(8,128)(2,1)S(1)}, u32[]{:S(2)}, u32[]{:S(2)}) collective-permute-start(bf16[128,2560]{1,0:T(8,128)(2,1)} %bitcast.73), channel_id=1, source_target_pairs={{0,4},{1,5},{2,6},{3,7},{4,8},{5,9},{6,10},{7,11},{8,12},{9,13},{1... | collective-permute-start | bytes 1966088 | tf_op jit(solution)/shard_map/ppermute | solution.py:44
  4.8 3.4 %collective-permute-start.1 = (bf16[128,2560]{1,0:T(8,128)(2,1)}, bf16[128,2560]{1,0:T(8,128)(2,1)S(1)}, u32[]{:S(2)}, u32[]{:S(2)}) collective-permute-start(bf16[128,2560]{1,0:T(8,128)(2,1)} %bitcast.74), channel_id=1, source_target_pairs={{0,12},{1,13},{2,14},{3,15},{4,0},{5,1},{6,2},{7,3},{8,4},{9,5},{1... | collective-permute-start | bytes 1966088 | tf_op jit(solution)/shard_map/ppermute | solution.py:45
  8.2 15.4 %collective-permute-start.3 = (bf16[128,2560]{1,0:T(8,128)(2,1)}, bf16[128,2560]{1,0:T(8,128)(2,1)}, u32[]{:S(2)}, u32[]{:S(2)}) collective-permute-start(bf16[128,2560]{1,0:T(8,128)(2,1)} %bitcast.75), channel_id=1, source_target_pairs={{0,2},{1,3},{2,0},{3,1},{4,6},{5,7},{6,4},{7,5},{8,10},{9,11},{10,... | collective-permute-start | bytes 1966088 | tf_op jit(solution)/shard_map/ppermute | solution.py:228
  25.0 2.1 collective-permute-start.4
  27.2 4.7 %collective-permute-start.5 = (bf16[64,2560]{1,0:T(8,128)(2,1)S(1)}, bf16[64,2560]{1,0:T(8,128)(2,1)}, u32[]{:S(2)}, u32[]{:S(2)}) collective-permute-start(bf16[64,2560]{1,0:T(8,128)(2,1)S(1)} %slice.46), channel_id=1, source_target_pairs={{0,12},{1,13},{2,14},{3,15},{4,0},{5,1},{6,2},{7,3},{8,4},{9,5},{1... | collective-permute-start | bytes 983048 | tf_op jit(solution)/shard_map/ppermute | solution.py:48
  34.7 3.9 %collective-permute-start.2 = (bf16[2560,384]{1,0:T(8,128)(2,1)}, bf16[2560,384]{1,0:T(8,128)(2,1)}, u32[]{:S(2)}, u32[]{:S(2)}) collective-permute-start(bf16[2560,384]{1,0:T(8,128)(2,1)} %constant_dynamic-update-slice_fusion.w_mine), channel_id=1, source_target_pairs={{0,1},{1,0},{2,3},{3,2},{4,5},{5,4},{6,7},{7,6},{8,9},{9,8},{10,11... | collective-permute-start | bytes 5898248 | tf_op jit(solution)/shard_map/ppermute | solution.py:232
  39.2 1.8 collective-permute-done.3
  41.1 2.8 %broadcast_in_dim.80 = bf16[4,128,2560]{2,1,0:T(8,128)(2,1)} broadcast(bf16[128,2560]{1,0:T(8,128)(2,1)} %collective-permute-done.3), dimensions={1,2} | broadcast | bytes 3276800 | tf_op jit(solution)/shard_map/broadcast_in_dim | solution.py:213
  43.9 8.6 %all-to-all-start = ((bf16[4,128,2560]{2,1,0:T(8,128)(2,1)}), bf16[4,128,2560]{2,1,0:T(8,128)(2,1)S(1)}, u32[]{:S(2)}, u32[]{:S(2)}) async-start(bf16[4,128,2560]{2,1,0:T(8,128)(2,1)} %broadcast_in_dim.80), calls=%async_computation | async-start | bytes 5242880 | tf_op jit(solution)/shard_map/all_to_all | solution.py:214
  59.8 8.5 %project.2 = (f32[4,128,384]{2,1,0:T(8,128)S(1)}, f32[4,128,384]{2,1,0:T(8,128)}, f32[4,2,128]{2,1,0:T(2,128)S(1)}) custom-call(s32[4]{0:T(128)S(1)} %and_select_fusion.order_ref, f32[1,2560]{1,0:T(1,128)S(1)} %get-tuple-element.40.scale_ref, f32[1,2560]{1,0:T(1,128)S(1)} %get-tuple-element.39.shift_ref, ...), custom_call_target="tpu_custom_call" | custom-call | flops 2013265920 | bytes 6553600 | tf_op jit(solution)/shard_map/project/pallas_call | solution.py:76
  69.2 4.8 %collective-permute-start.6 = (f32[4,128,384]{2,1,0:T(8,128)}, f32[4,128,384]{2,1,0:T(8,128)}, u32[]{:S(2)}, u32[]{:S(2)}) collective-permute-start(f32[4,128,384]{2,1,0:T(8,128)} %get-tuple-element.31), channel_id=1, source_target_pairs={{0,1},{1,0},{2,3},{3,2},{4,5},{5,4},{6,7},{7,6},{8,9},{9,8},{10,11... | collective-permute-start | bytes 2359304 | tf_op jit(solution)/shard_map/ppermute | solution.py:249
  74.1 7.5 %all-to-all-done = bf16[4,128,2560]{2,1,0:T(8,128)(2,1)S(1)} async-done(((bf16[4,128,2560]{2,1,0:T(8,128)(2,1)}), bf16[4,128,2560]{2,1,0:T(8,128)(2,1)S(1)}, u32[]{:S(2)}, u32[]{:S(2)}) %all-to-all-start) | async-done | bytes 2621472 | tf_op jit(solution)/shard_map/all_to_all | solution.py:214
  81.5 8.5 %project.3 = (f32[4,128,384]{2,1,0:T(8,128)S(1)}, f32[4,128,384]{2,1,0:T(8,128)}, f32[4,2,128]{2,1,0:T(2,128)S(1)}) custom-call(s32[4]{0:T(128)S(1)} %iota.22.order_ref, f32[1,2560]{1,0:T(1,128)S(1)} %get-tuple-element.40.scale_ref, f32[1,2560]{1,0:T(1,128)S(1)} %get-tuple-element.39.shift_ref, bf16[2560,384]{1,0:T(8,128)(2,1)} %constant_dynamic-update-slice_fusion.w_mine, ...), custom_call_target="tpu_custom_call" | custom-call | flops 2013265920 | bytes 6553600 | tf_op jit(solution)/shard_map/project/pallas_call | solution.py:76
  90.9 5.7 %collective-permute-start.7 = (f32[4,128,384]{2,1,0:T(8,128)}, f32[4,128,384]{2,1,0:T(8,128)S(1)}, u32[]{:S(2)}, u32[]{:S(2)}) collective-permute-start(f32[4,128,384]{2,1,0:T(8,128)} %get-tuple-element.32), channel_id=1, source_target_pairs={{0,1},{1,0},{2,3},{3,2},{4,5},{5,4},{6,7},{7,6},{8,9},{9,8},{10,11... | collective-permute-start | bytes 2359304 | tf_op jit(solution)/shard_map/ppermute | solution.py:249
  97.3 13.2 %all-to-all-start.1 = ((f32[16,16,128]{2,1,0:T(8,128)}), f32[16,16,128]{2,1,0:T(8,128)S(1)}, u32[]{:S(2)}, u32[]{:S(2)}) async-start(f32[16,16,128]{2,1,0:T(8,128)} %broadcast_in_dim.82), calls=%async_computation.1 | async-start | bytes 262144 | tf_op jit(solution)/shard_map/all_to_all | solution.py:214
  112.6 12.8 %all-to-all-done.1.power_ref = f32[16,16,128]{2,1,0:T(8,128)S(1)} async-done(((f32[16,16,128]{2,1,0:T(8,128)}), f32[16,16,128]{2,1,0:T(8,128)S(1)}, u32[]{:S(2)}, u32[]{:S(2)}) %all-to-all-start.1) | async-done | bytes 131104 | tf_op jit(solution)/shard_map/all_to_all | solution.py:214
  126.4 15.3 %attend.1 = bf16[4,2,2,64,128]{4,3,2,1,0:T(8,128)(2,1)} custom-call(s32[4]{0:T(128)} %pad_add_fusion.place_ref, f32[16,16,128]{2,1,0:T(8,128)} %copy-done.11, f32[2,128]{1,0:T(2,128)} %gain_ref.1, bf16[2048,64]{1,0:T(8,128)(2,1)} %copy.21.w_head_ref, f32[4,128,384]{2,1,0:T(8,128)} %copy-done.1, f32[4,128,384]{2,1,0:T(8,128)} %copy-done.2, ...), custom_call_target="tpu_custom_call" | custom-call | flops 4294967296 | bytes 4194304 | tf_op jit(solution)/shard_map/attend/pallas_call | solution.py:178
  141.7 4.1 %all-to-all-start.2 = ((bf16[8,2,64,128]{3,2,1,0:T(8,128)(2,1)}), bf16[8,2,64,128]{3,2,1,0:T(8,128)(2,1)S(1)}, u32[]{:S(2)}, u32[]{:S(2)}) async-start(bf16[8,2,64,128]{3,2,1,0:T(8,128)(2,1)} %bitcast.77), calls=%async_computation.2 | async-start | bytes 524288 | tf_op jit(solution)/shard_map/all_to_all | solution.py:265
  145.7 6.5 %all-to-all-done.2 = bf16[8,2,64,128]{3,2,1,0:T(8,128)(2,1)S(1)} async-done(((bf16[8,2,64,128]{3,2,1,0:T(8,128)(2,1)}), bf16[8,2,64,128]{3,2,1,0:T(8,128)(2,1)S(1)}, u32[]{:S(2)}, u32[]{:S(2)}) %all-to-all-start.2) | async-done | bytes 262176 | tf_op jit(solution)/shard_map/all_to_all | solution.py:265
  153.7 38.1 %all-to-all-start.3 = ((bf16[16,64,128]{2,1,0:T(8,128)(2,1)}), bf16[16,64,128]{2,1,0:T(8,128)(2,1)S(1)}, u32[]{:S(2)}, u32[]{:S(2)}) async-start(bf16[16,64,128]{2,1,0:T(8,128)(2,1)} %bitcast.19), calls=%async_computation.3 | async-start | bytes 524288 | tf_op jit(solution)/shard_map/all_to_all | solution.py:271
  197.5 7.2 %all-to-all-done.3 = bf16[16,64,128]{2,1,0:T(8,128)(2,1)S(1)} async-done(((bf16[16,64,128]{2,1,0:T(8,128)(2,1)}), bf16[16,64,128]{2,1,0:T(8,128)(2,1)S(1)}, u32[]{:S(2)}, u32[]{:S(2)}) %all-to-all-start.3) | async-done | bytes 262176 | tf_op jit(solution)/shard_map/all_to_all | solution.py:271
  205.6 4.0 %all-to-all-start.4 = ((f32[4,64,128]{2,1,0:T(8,128)}), f32[4,64,128]{2,1,0:T(8,128)S(1)}, u32[]{:S(2)}, u32[]{:S(2)}) async-start(f32[4,64,128]{2,1,0:T(8,128)} %broadcast_in_dim.90), calls=%async_computation.4 | async-start | bytes 262144 | tf_op jit(solution)/shard_map/all_to_all | solution.py:214
  209.6 4.8 %all-to-all-done.4 = f32[4,64,128]{2,1,0:T(8,128)S(1)} async-done(((f32[4,64,128]{2,1,0:T(8,128)}), f32[4,64,128]{2,1,0:T(8,128)S(1)}, u32[]{:S(2)}, u32[]{:S(2)}) %all-to-all-start.4) | async-done | bytes 131104 | tf_op jit(solution)/shard_map/all_to_all | solution.py:214
  216.4 28.1 %all_to_all.30 = f32[16,1,128]{2,1,0:T(1,128)S(1)} all-to-all(f32[16,1,128]{2,1,0:T(1,128)S(1)} %broadcast_in_dim_broadcast_in_dim_broadcast_in_dim.3), channel_id=1, replica_groups=mesh['tm'=32,'seq'=16] {'seq'}, dimensions={0} | all-to-all | bytes 16384 | tf_op jit(solution)/shard_map/all_to_all | solution.py:214
  (88 shorter events, 22.2 us)
Async XLA Ops:
  0.6 151.7 %copy-start = (bf16[2560,64]{0,1:T(8,128)(2,1)S(1)}, bf16[2560,64]{0,1:T(8,128)(2,1)}, u32[]{:S(2)}) copy-start(bf16[2560,64]{0,1:T(8,128)(2,1)} %param.23) | copy-start | bytes 983044
  0.6 31.2 %copy-start.7 = (bf16[2560,128]{1,0:T(8,128)(2,1)S(1)}, bf16[2560,128]{1,0:T(8,128)(2,1)}, u32[]{:S(2)}) copy-start(bf16[2560,128]{1,0:T(8,128)(2,1)} %param.18) | copy-start | bytes 1966084
  0.7 32.2 %copy-start.8 = (bf16[2560,128]{1,0:T(8,128)(2,1)S(1)}, bf16[2560,128]{1,0:T(8,128)(2,1)}, u32[]{:S(2)}) copy-start(bf16[2560,128]{1,0:T(8,128)(2,1)} %param.19) | copy-start | bytes 1966084
  0.7 24.3 %collective-permute-start = (bf16[128,2560]{1,0:T(8,128)(2,1)}, bf16[128,2560]{1,0:T(8,128)(2,1)S(1)}, u32[]{:S(2)}, u32[]{:S(2)}) collective-permute-start(bf16[128,2560]{1,0:T(8,128)(2,1)} %bitcast.73), channel_id=1, source_target_pairs={{0,4},{1,5},{2,6},{3,7},{4,8},{5,9},{6,10},{7,11},{8,12},{9,13},{1... | collective-permute-start | bytes 1966088 | tf_op jit(solution)/shard_map/ppermute | solution.py:44
  4.8 22.3 %collective-permute-start.1 = (bf16[128,2560]{1,0:T(8,128)(2,1)}, bf16[128,2560]{1,0:T(8,128)(2,1)S(1)}, u32[]{:S(2)}, u32[]{:S(2)}) collective-permute-start(bf16[128,2560]{1,0:T(8,128)(2,1)} %bitcast.74), channel_id=1, source_target_pairs={{0,12},{1,13},{2,14},{3,15},{4,0},{5,1},{6,2},{7,3},{8,4},{9,5},{1... | collective-permute-start | bytes 1966088 | tf_op jit(solution)/shard_map/ppermute | solution.py:45
  8.2 32.9 %collective-permute-start.3 = (bf16[128,2560]{1,0:T(8,128)(2,1)}, bf16[128,2560]{1,0:T(8,128)(2,1)}, u32[]{:S(2)}, u32[]{:S(2)}) collective-permute-start(bf16[128,2560]{1,0:T(8,128)(2,1)} %bitcast.75), channel_id=1, source_target_pairs={{0,2},{1,3},{2,0},{3,1},{4,6},{5,7},{6,4},{7,5},{8,10},{9,11},{10,... | collective-permute-start | bytes 1966088 | tf_op jit(solution)/shard_map/ppermute | solution.py:228
  25.0 8.8 %copy-start.9 = (bf16[2560,128]{1,0:T(8,128)(2,1)S(1)}, bf16[2560,128]{1,0:T(8,128)(2,1)}, u32[]{:S(2)}) copy-start(bf16[2560,128]{1,0:T(8,128)(2,1)} %param.20) | copy-start | bytes 1966084
  25.0 8.8 %copy-start.4 = (bf16[128,2560]{1,0:T(8,128)(2,1)}, bf16[128,2560]{1,0:T(8,128)(2,1)S(1)}, u32[]{:S(2)}) copy-start(bf16[128,2560]{1,0:T(8,128)(2,1)S(1)} %collective-permute-done) | copy-start | bytes 1966084
  25.0 16.0 %collective-permute-start.4 = (bf16[64,2560]{1,0:T(8,128)(2,1)S(1)}, bf16[64,2560]{1,0:T(8,128)(2,1)S(1)}, u32[]{:S(2)}, u32[]{:S(2)}) collective-permute-start(bf16[64,2560]{1,0:T(8,128)(2,1)S(1)} %slice.45), channel_id=1, source_target_pairs={{0,4},{1,5},{2,6},{3,7},{4,8},{5,9},{6,10},{7,11},{8,12},{9,13},{1... | collective-permute-start | bytes 983048 | tf_op jit(solution)/shard_map/ppermute | solution.py:48
  27.1 11.5 %copy-start.15 = (s32[32]{0:T(128)S(1)}, s32[32]{0:T(128)}, u32[]{:S(2)}) copy-start(s32[32]{0:T(128)} %param.16) | copy-start | bytes 388
  27.2 13.9 %collective-permute-start.5 = (bf16[64,2560]{1,0:T(8,128)(2,1)S(1)}, bf16[64,2560]{1,0:T(8,128)(2,1)}, u32[]{:S(2)}, u32[]{:S(2)}) collective-permute-start(bf16[64,2560]{1,0:T(8,128)(2,1)S(1)} %slice.46), channel_id=1, source_target_pairs={{0,12},{1,13},{2,14},{3,15},{4,0},{5,1},{6,2},{7,3},{8,4},{9,5},{1... | collective-permute-start | bytes 983048 | tf_op jit(solution)/shard_map/ppermute | solution.py:48
  34.7 25.1 %collective-permute-start.2 = (bf16[2560,384]{1,0:T(8,128)(2,1)}, bf16[2560,384]{1,0:T(8,128)(2,1)}, u32[]{:S(2)}, u32[]{:S(2)}) collective-permute-start(bf16[2560,384]{1,0:T(8,128)(2,1)} %constant_dynamic-update-slice_fusion.w_mine), channel_id=1, source_target_pairs={{0,1},{1,0},{2,3},{3,2},{4,5},{5,4},{6,7},{7,6},{8,9},{9,8},{10,11... | collective-permute-start | bytes 5898248 | tf_op jit(solution)/shard_map/ppermute | solution.py:232
  43.9 9.9 %copy-start.10 = (bf16[2048,64]{0,1:T(8,128)(2,1)S(1)}, bf16[2048,64]{0,1:T(8,128)(2,1)}, u32[]{:S(2)}) copy-start(bf16[2048,64]{0,1:T(8,128)(2,1)} %param.22) | copy-start | bytes 786436
  43.9 37.6 %all-to-all-start = ((bf16[4,128,2560]{2,1,0:T(8,128)(2,1)}), bf16[4,128,2560]{2,1,0:T(8,128)(2,1)S(1)}, u32[]{:S(2)}, u32[]{:S(2)}) async-start(bf16[4,128,2560]{2,1,0:T(8,128)(2,1)} %broadcast_in_dim.80), calls=%async_computation | async-start | bytes 5242880 | tf_op jit(solution)/shard_map/all_to_all | solution.py:214
  69.2 43.4 %collective-permute-start.6 = (f32[4,128,384]{2,1,0:T(8,128)}, f32[4,128,384]{2,1,0:T(8,128)}, u32[]{:S(2)}, u32[]{:S(2)}) collective-permute-start(f32[4,128,384]{2,1,0:T(8,128)} %get-tuple-element.31), channel_id=1, source_target_pairs={{0,1},{1,0},{2,3},{3,2},{4,5},{5,4},{6,7},{7,6},{8,9},{9,8},{10,11... | collective-permute-start | bytes 2359304 | tf_op jit(solution)/shard_map/ppermute | solution.py:249
  90.9 34.5 %collective-permute-start.7 = (f32[4,128,384]{2,1,0:T(8,128)}, f32[4,128,384]{2,1,0:T(8,128)S(1)}, u32[]{:S(2)}, u32[]{:S(2)}) collective-permute-start(f32[4,128,384]{2,1,0:T(8,128)} %get-tuple-element.32), channel_id=1, source_target_pairs={{0,1},{1,0},{2,3},{3,2},{4,5},{5,4},{6,7},{7,6},{8,9},{9,8},{10,11... | collective-permute-start | bytes 2359304 | tf_op jit(solution)/shard_map/ppermute | solution.py:249
  97.3 28.1 %all-to-all-start.1 = ((f32[16,16,128]{2,1,0:T(8,128)}), f32[16,16,128]{2,1,0:T(8,128)S(1)}, u32[]{:S(2)}, u32[]{:S(2)}) async-start(f32[16,16,128]{2,1,0:T(8,128)} %broadcast_in_dim.82), calls=%async_computation.1 | async-start | bytes 262144 | tf_op jit(solution)/shard_map/all_to_all | solution.py:214
  126.4 25.9 %copy-start.3 = (bf16[1,128,2560]{2,1,0:T(8,128)(2,1)S(1)}, bf16[1,128,2560]{2,1,0:T(8,128)(2,1)}, u32[]{:S(2)}) copy-start(bf16[1,128,2560]{2,1,0:T(8,128)(2,1)} %param.14) | copy-start | bytes 1966084
  141.7 52.9 %copy-start.14 = (f32[51]{0:T(128)S(1)}, f32[51]{0:T(128)}, u32[]{:S(2)}) copy-start(f32[51]{0:T(128)} %param.17) | copy-start | bytes 616
  141.7 10.6 %all-to-all-start.2 = ((bf16[8,2,64,128]{3,2,1,0:T(8,128)(2,1)}), bf16[8,2,64,128]{3,2,1,0:T(8,128)(2,1)S(1)}, u32[]{:S(2)}, u32[]{:S(2)}) async-start(bf16[8,2,64,128]{3,2,1,0:T(8,128)(2,1)} %bitcast.77), calls=%async_computation.2 | async-start | bytes 524288 | tf_op jit(solution)/shard_map/all_to_all | solution.py:265
  152.8 61.7 %copy-start.12 = (f32[1,128,64]{1,2,0:T(8,128)S(1)}, f32[1,128,64]{1,2,0:T(8,128)}, u32[]{:S(2)}) copy-start(f32[1,128,64]{1,2,0:T(8,128)} %param.13) | copy-start | bytes 98308
  152.8 61.7 %copy-start.13 = (f32[128,64]{0,1:T(8,128)S(1)}, f32[128,64]{0,1:T(8,128)}, u32[]{:S(2)}) copy-start(f32[128,64]{0,1:T(8,128)} %param.12) | copy-start | bytes 98308
  153.7 51.0 %all-to-all-start.3 = ((bf16[16,64,128]{2,1,0:T(8,128)(2,1)}), bf16[16,64,128]{2,1,0:T(8,128)(2,1)S(1)}, u32[]{:S(2)}, u32[]{:S(2)}) async-start(bf16[16,64,128]{2,1,0:T(8,128)(2,1)} %bitcast.19), calls=%async_computation.3 | async-start | bytes 524288 | tf_op jit(solution)/shard_map/all_to_all | solution.py:271
  205.6 8.8 %all-to-all-start.4 = ((f32[4,64,128]{2,1,0:T(8,128)}), f32[4,64,128]{2,1,0:T(8,128)S(1)}, u32[]{:S(2)}, u32[]{:S(2)}) async-start(f32[4,64,128]{2,1,0:T(8,128)} %broadcast_in_dim.90), calls=%async_computation.4 | async-start | bytes 262144 | tf_op jit(solution)/shard_map/all_to_all | solution.py:214
  (6 other events, 14.2 us)

commit v3 on v2

--- a/solution.py
+++ b/solution.py
@@ -34,45 +34,38 @@
 TO_CORE = seq_perm(lambda y, z, c: (y, z, 1 - c))
 Y_GROUPS = [[y * Z * C + r for y in range(Y)] for r in range(Z * C)]
 YC_GROUPS = [[(y * Z + z) * C + c for y in range(Y) for c in range(C)] for z in range(Z)]
-TO_UP = seq_perm(lambda y, z, c: (y + 1, z, c))
-TO_DOWN = seq_perm(lambda y, z, c: (y - 1, z, c))
+CHUNKS = ((0, 128),)
 TO_FAR = seq_perm(lambda y, z, c: (y, 1 - z, c))
 
 
-def along_y(rows):
-    half = rows.shape[0] // 2
-    below = lax.ppermute(rows, "seq", TO_UP)
-    above = lax.ppermute(rows, "seq", TO_DOWN)
-    return (
-        rows, below, above,
-        lax.ppermute(below[:half], "seq", TO_UP), lax.ppermute(above[half:], "seq", TO_DOWN),
-    )
-
-
 def project_kernel(
-    order_ref, scale_ref, shift_ref, w_mine, w_theirs, rows_ref, mine_ref, other_ref, power_ref
+    scale_ref, shift_ref, w_mine, w_theirs, rows_ref, mine_ref, other_ref, power_ref, normed_ref
 ):
     rows = rows_ref[...].astype(jnp.float32)
     average = jnp.mean(rows, axis=-1, keepdims=True)
     centred = rows - average
     spread = jnp.mean(centred * centred, axis=-1, keepdims=True)
     normed = centred * lax.rsqrt(spread + 1e-6) * (1.0 + scale_ref[...]) + shift_ref[...]
-    normed = normed.astype(jnp.bfloat16)
-    mine = jnp.dot(normed, w_mine[...], preferred_element_type=jnp.float32)
-    other = jnp.dot(normed, w_theirs[...], preferred_element_type=jnp.float32)
-    mine_ref[0] = mine
-    other_ref[0] = other
-    for part in range(2):
-        cols = slice(part * 128, (part + 1) * 128)
-        squares = mine[:, cols] * mine[:, cols] + other[:, cols] * other[:, cols]
-        power_ref[0, part : part + 1, :] = jnp.sum(jnp.transpose(squares), axis=0, keepdims=True)
-
-
-def project(order, scale, shift, w_mine, w_theirs, rows):
+    normed_ref[...] = normed.astype(jnp.bfloat16)
+    mine = jnp.dot(normed_ref[...], w_mine[...], preferred_element_type=jnp.float32)
+    other = jnp.dot(normed_ref[...], w_theirs[...], preferred_element_type=jnp.float32)
+    count = mine.shape[0] // Y
+    for y in range(Y):
+        rows = slice(y * count, (y + 1) * count)
+        mine_ref[y] = mine[rows]
+        other_ref[y] = other[rows]
+        for part in range(2):
+            cols = slice(part * 128, (part + 1) * 128)
+            squares = mine[rows, cols] * mine[rows, cols] + other[rows, cols] * other[rows, cols]
+            power_ref[y, part : part + 1, :] = jnp.sum(
+                jnp.transpose(squares), axis=0, keepdims=True
+            )
+
+
+def project(scale, shift, w_mine, w_theirs, rows):
     features, columns = w_mine.shape
     count = rows.shape[0] // Y
     vmem = pl.BlockSpec(memory_space=pltpu.VMEM)
-    stack = pl.BlockSpec((1, count, columns), lambda y, order: (order[y], 0, 0))
     return pl.pallas_call(
         project_kernel,
         out_shape=(
@@ -80,12 +73,9 @@
             jax.ShapeDtypeStruct((Y, count, columns), jnp.float32),
             jax.ShapeDtypeStruct((Y, 2, count), jnp.float32),
         ),
-        grid_spec=pltpu.PrefetchScalarGridSpec(
-            num_scalar_prefetch=1,
-            grid=(Y,),
-            in_specs=[vmem, vmem, vmem, vmem, pl.BlockSpec((count, features), lambda y, order: (y, 0))],
-            out_specs=(stack, stack, pl.BlockSpec((1, 2, count), lambda y, order: (order[y], 0, 0))),
-        ),
+        in_specs=[vmem] * 5,
+        out_specs=(vmem, vmem, vmem),
+        scratch_shapes=[pltpu.VMEM(rows.shape, jnp.bfloat16)],
         compiler_params=pltpu.CompilerParams(vmem_limit_bytes=24 * 2**20),
         cost_estimate=pl.CostEstimate(
             flops=2 * Y * count * features * 768,
@@ -93,7 +83,7 @@
             transcendentals=0,
         ),
         name="project",
-    )(order, scale, shift, w_mine, w_theirs, rows)
+    )(scale, shift, w_mine, w_theirs, rows)
 
 
 def attend_kernel(chunks, place_ref, power_ref, gain_ref, w_head_ref, *refs):
@@ -225,11 +215,16 @@
     place = jnp.stack([my_y, my_z, my_c, seq_rank])
     raw = hidden[0]
 
-    far = lax.ppermute(raw, "seq", TO_FAR)
-    own = along_y(raw)
-    w_parts, _ = lax.optimization_barrier(((w_query, w_key, w_value), own[1:3]))
-    w_mine = jnp.concatenate(w_parts, axis=1)
+    far = [lax.ppermute(raw[a:b], "seq", TO_FAR) for a, b in CHUNKS]
+
+    once = lax.optimization_barrier(jnp.int32(1))
+    own = lax.fori_loop(
+        0, once, lambda _, own: spread_over(raw, "seq", Y, Y_GROUPS), jnp.zeros((Y,) + raw.shape, raw.dtype)
+    )
+    parts, own = lax.optimization_barrier(((w_query, w_key, w_value), own))
+    w_mine = jnp.concatenate(parts, axis=1)
     w_theirs = lax.ppermute(w_mine, "seq", TO_CORE)
+    own = own.reshape(-1, raw.shape[1])
     following = jnp.concatenate([step_index[1:], step_index[-1:] + 1])
     step_now = lax.dynamic_index_in_dim(step_index, time_rank, 0, False)
     step_next = lax.dynamic_index_in_dim(following, time_rank, 0, False)
@@ -243,23 +238,29 @@
 
     mine, theirs, powers = [], [], []
 
-    def project_stack(order, rows):
-        kept, given, power = project(order, scale, shift, w_mine, w_theirs, rows)
+    def project_stack(rows):
+        kept, given, power = project(scale, shift, w_mine, w_theirs, rows)
         mine.append(kept)
         theirs.append(lax.ppermute(given, "seq", TO_CORE))
         powers.append(power)
 
-    far, own = lax.optimization_barrier((far, own))
-    far = spread_over(far, "seq", Y, Y_GROUPS).reshape(-1, raw.shape[1])
-    project_stack(jnp.stack([my_y, my_y + 3, my_y + 1, my_y + 2]) % Y, jnp.concatenate(own))
-    project_stack(jnp.arange(Y, dtype=jnp.int32), far)
-    power_own, power_far = powers
+    project_stack(own)
+    for at, rows in enumerate(far):
+        if at > 0:
+            rows, stack = lax.optimization_barrier((rows, stack))
+            project_stack(stack)
+        else:
+            rows, _ = lax.optimization_barrier((rows, own))
+        stack = spread_over(rows, "seq", Y, Y_GROUPS).reshape(-1, raw.shape[1])
+    stack, _ = lax.optimization_barrier((stack, powers))
+    project_stack(stack)
+    power_own, power_far = powers[0], jnp.concatenate(powers[1:], axis=2)
     low = jnp.where(my_z == 0, power_own, power_far)
     high = jnp.where(my_z == 0, power_far, power_own)
     table = jnp.stack([low, high], axis=1).transpose(2, 0, 1, 3).reshape(2 * Y * Z, 128)
     powers = spread_over(table, "seq", Y * Z * C)
 
-    chunks = ((0, 0, 128), (1, 0, 128))
+    chunks = ((0, 0, 128),) + tuple((1, a, b) for a, b in CHUNKS)
     partial = attend(chunks, place, powers, qk_gain, w_head, mine, theirs)
     partial = partial.reshape(Y * C, Z, LAT, 128)
     partial = lax.all_to_all(partial, "seq", 0, 0, axis_index_groups=YC_GROUPS)

time: 248 us -> 239 us (0.964)
  starting transfers between devices: 112 us -> 69.6 us
  waiting for transfers between devices: 40.7 us -> 77.8 us
    all_to_all x3 -> x4, waiting for transfers between devices: 25.1 us -> 64.1 us  [spread_over(): return lax.all_to_all(copies, axis, 0, 0, axis_index_groups=groups)]
    ppermute x5 -> x1, starting transfers between devices: 29.7 us -> 16.4 us  [per_device(): far = [lax.ppermute(raw[a:b], 'seq', TO_FAR) for a, b in CHUNKS]]
    all_to_all x1, starting transfers between devices: 38.1 us -> 24.8 us  [per_device(): line = lax.all_to_all(sent, ('tm', 'seq'), 0, 0, axis_index_groups=Z_GROUPS)]
    all_to_all x3 -> x4, starting transfers between devices: 25.8 us -> 15.9 us  [spread_over(): return lax.all_to_all(copies, axis, 0, 0, axis_index_groups=groups)]
    ppermute x2, starting transfers between devices: 10.5 us -> 4.59 us  [project_stack(): theirs.append(lax.ppermute(given, 'seq', TO_CORE))]
    unnamed x41 -> x33, local copies, waits for them, and re-layouts: 8.07 us -> 5.74 us
  transfers between devices with their start and end apart: 13 -> 10, of which waited for: 6 -> 6; matrix products, arithmetic and copies ran while one was open for 7% -> 7% of each run, Pallas kernels for 7% -> 6%
where the time goes in v3:
time: 239 us; the launch traced here: 238 us
  waiting for transfers between devices  77.8 us (33%)
  starting transfers between devices  69.6 us (29%)
  Pallas kernels  30.4 us (13%)
  blocking collectives  28.1 us (12%)
  local copies, waits for them, and re-layouts  16.4 us (7%)
  between operations  8.66 us (4%)
  other arithmetic  6.63 us (3%)
    all_to_all x4, waiting for transfers between devices, spread_over(): return lax.all_to_all(copies, axis, 0, 0, axis_index_groups=groups)  64.1 us
    all_to_all x1, blocking collectives, spread_over(): return lax.all_to_all(copies, axis, 0, 0, axis_index_groups=groups)  28.1 us
    all_to_all x1, starting transfers between devices, per_device(): line = lax.all_to_all(sent, ('tm', 'seq'), 0, 0, axis_index_groups=Z_GROUPS)  24.8 us
    ppermute x1, starting transfers between devices, per_device(): far = [lax.ppermute(raw[a:b], 'seq', TO_FAR) for a, b in CHUNKS]  16.4 us
    all_to_all x4, starting transfers between devices, spread_over(): return lax.all_to_all(copies, axis, 0, 0, axis_index_groups=groups)  15.9 us
    pallas_call x1, Pallas kernels, attend(): pl.pallas_call(functools.partial(attend_kernel, chunks), out_shape=jax.Sh...  15.2 us
    pallas_call x2, Pallas kernels, project(): pl.pallas_call(project_kernel, out_shape=(jax.ShapeDtypeStruct((Y, count,...  15.1 us
    all_to_all x1, waiting for transfers between devices, per_device(): line = lax.all_to_all(sent, ('tm', 'seq'), 0, 0, axis_index_groups=Z_GROUPS)  7.22 us
  transfers between devices with their start and end apart: 10, of which 6 were waited for; matrix products, arithmetic and copies ran while one was open for 7% of the time, Pallas kernels for 6%

profile of v3, /device:TPU:1, one launch (start us, length us, event | category | flops | bytes accessed | tf_op | source)
XLA Modules:
  0.0 238.3 jit_solution(7426237273608366392)
XLA Ops:
  0.7 16.4 %collective-permute-start.1 = (bf16[128,2560]{1,0:T(8,128)(2,1)}, bf16[128,2560]{1,0:T(8,128)(2,1)S(1)}, u32[]{:S(2)}, u32[]{:S(2)}) collective-permute-start(bf16[128,2560]{1,0:T(8,128)(2,1)} %bitcast.74), channel_id=1, source_target_pairs={{0,2},{1,3},{2,0},{3,1},{4,6},{5,7},{6,4},{7,5},{8,10},{9,11},{10,... | collective-permute-start | bytes 1966088 | tf_op jit(solution)/shard_map/ppermute | solution.py:218
  17.1 1.7 broadcast_in_dim.90
  18.8 37.4 %while.10 = (s32[]{:T(128)}, bf16[4,128,2560]{2,1,0:T(8,128)(2,1)}, s32[]{:T(128)}, bf16[1,128,2560]{2,1,0:T(8,128)(2,1)S(1)}, s32[]{:T(128)}) while((s32[]{:T(128)}, bf16[4,128,2560]{2,1,0:T(8,128)(2,1)}, s32[]{:T(128)}, bf16[1,128,2560]{2,1,0:T(8,128)(2,1)S(1)}, s32[]{:T(128)}) %tuple.40), condition=%wide.region_1.2_spmd, body=%wide.region_0.1_spmd.sunk | while | flops 2 | bytes 11141213 | solution.py:221
  18.8 1.7 broadcast_in_dim.111
  20.5 4.6 %all-to-all-start = ((bf16[4,128,2560]{2,1,0:T(8,128)(2,1)}), bf16[4,128,2560]{2,1,0:T(8,128)(2,1)}, u32[]{:S(2)}, u32[]{:S(2)}) async-start(bf16[4,128,2560]{2,1,0:T(8,128)(2,1)} %broadcast_in_dim.111), calls=%async_computation | async-start | bytes 5242880 | tf_op jit(solution)/shard_map/while/body/all_to_all | solution.py:204
  25.1 31.1 %all-to-all-done = bf16[4,128,2560]{2,1,0:T(8,128)(2,1)} async-done(((bf16[4,128,2560]{2,1,0:T(8,128)(2,1)}), bf16[4,128,2560]{2,1,0:T(8,128)(2,1)}, u32[]{:S(2)}, u32[]{:S(2)}) %all-to-all-start) | async-done | bytes 2621472 | tf_op jit(solution)/shard_map/while/body/all_to_all | solution.py:204
  59.1 3.8 %collective-permute-start = (bf16[2560,384]{1,0:T(8,128)(2,1)}, bf16[2560,384]{1,0:T(8,128)(2,1)}, u32[]{:S(2)}, u32[]{:S(2)}) collective-permute-start(bf16[2560,384]{1,0:T(8,128)(2,1)} %constant_dynamic-update-slice_fusion.w_mine), channel_id=1, source_target_pairs={{0,1},{1,0},{2,3},{3,2},{4,5},{5,4},{6,7},{7,6},{8,9},{9,8},{10,11... | collective-permute-start | bytes 5898248 | tf_op jit(solution)/shard_map/ppermute | solution.py:226
  62.9 1.7 broadcast_in_dim.91
  64.6 3.8 %all-to-all-start.1 = ((bf16[4,128,2560]{2,1,0:T(8,128)(2,1)}), bf16[4,128,2560]{2,1,0:T(8,128)(2,1)S(1)}, u32[]{:S(2)}, u32[]{:S(2)}) async-start(bf16[4,128,2560]{2,1,0:T(8,128)(2,1)} %broadcast_in_dim.91), calls=%async_computation.1 | async-start | bytes 5242880 | tf_op jit(solution)/shard_map/all_to_all | solution.py:204
  74.2 7.9 %project.2 = (f32[4,128,384]{2,1,0:T(8,128)S(1)}, f32[4,128,384]{2,1,0:T(8,128)}, f32[4,2,128]{2,1,0:T(2,128)S(1)}) custom-call(f32[1,2560]{1,0:T(1,128)S(1)} %get-tuple-element.65.scale_ref, f32[1,2560]{1,0:T(1,128)S(1)} %get-tuple-element.64.shift_ref, bf16[2560,384]{1,0:T(8,128)(2,1)} %constant_dynamic-update-slice_fusion.w_mine, ...), custom_call_target="tpu_custom_call" | custom-call | flops 2013265920 | bytes 6553600 | tf_op jit(solution)/shard_map/project/pallas_call | solution.py:69
  83.0 1.9 collective-permute-start.2
  84.9 15.5 %all-to-all-done.1 = bf16[4,128,2560]{2,1,0:T(8,128)(2,1)S(1)} async-done(((bf16[4,128,2560]{2,1,0:T(8,128)(2,1)}), bf16[4,128,2560]{2,1,0:T(8,128)(2,1)S(1)}, u32[]{:S(2)}, u32[]{:S(2)}) %all-to-all-start.1) | async-done | bytes 2621472 | tf_op jit(solution)/shard_map/all_to_all | solution.py:204
  100.5 7.2 %project.3 = (f32[4,128,384]{2,1,0:T(8,128)S(1)}, f32[4,128,384]{2,1,0:T(8,128)}, f32[4,2,128]{2,1,0:T(2,128)S(1)}) custom-call(f32[1,2560]{1,0:T(1,128)S(1)} %get-tuple-element.65.scale_ref, f32[1,2560]{1,0:T(1,128)S(1)} %get-tuple-element.64.shift_ref, bf16[2560,384]{1,0:T(8,128)(2,1)} %constant_dynamic-update-slice_fusion.w_mine, ...), custom_call_target="tpu_custom_call" | custom-call | flops 2013265920 | bytes 6553600 | tf_op jit(solution)/shard_map/project/pallas_call | solution.py:69
  108.6 2.7 %collective-permute-start.3 = (f32[4,128,384]{2,1,0:T(8,128)}, f32[4,128,384]{2,1,0:T(8,128)S(1)}, u32[]{:S(2)}, u32[]{:S(2)}) collective-permute-start(f32[4,128,384]{2,1,0:T(8,128)} %get-tuple-element.49), channel_id=1, source_target_pairs={{0,1},{1,0},{2,3},{3,2},{4,5},{5,4},{6,7},{7,6},{8,9},{9,8},{10,11... | collective-permute-start | bytes 2359304 | tf_op jit(solution)/shard_map/ppermute | solution.py:244
  111.9 3.6 %all-to-all-start.2 = ((f32[16,16,128]{2,1,0:T(8,128)}), f32[16,16,128]{2,1,0:T(8,128)S(1)}, u32[]{:S(2)}, u32[]{:S(2)}) async-start(f32[16,16,128]{2,1,0:T(8,128)} %broadcast_in_dim.93), calls=%async_computation.2 | async-start | bytes 262144 | tf_op jit(solution)/shard_map/all_to_all | solution.py:204
  117.6 12.6 %all-to-all-done.2.power_ref = f32[16,16,128]{2,1,0:T(8,128)S(1)} async-done(((f32[16,16,128]{2,1,0:T(8,128)}), f32[16,16,128]{2,1,0:T(8,128)S(1)}, u32[]{:S(2)}, u32[]{:S(2)}) %all-to-all-start.2) | async-done | bytes 131104 | tf_op jit(solution)/shard_map/all_to_all | solution.py:204
  131.2 15.2 %attend.1 = bf16[4,2,2,64,128]{4,3,2,1,0:T(8,128)(2,1)} custom-call(s32[4]{0:T(128)} %pad_add_fusion.place_ref, f32[16,16,128]{2,1,0:T(8,128)} %copy-done.9, f32[2,128]{1,0:T(2,128)} %gain_ref.1, bf16[2048,64]{1,0:T(8,128)(2,1)} %copy.21.w_head_ref, f32[4,128,384]{2,1,0:T(8,128)} %copy-done.1, f32[4,128,384]{2,1,0:T(8,128)} %copy-done.2, ...), custom_call_target="tpu_custom_call" | custom-call | flops 4294967296 | bytes 4194304 | tf_op jit(solution)/shard_map/attend/pallas_call | solution.py:168
  146.4 4.1 %all-to-all-start.3 = ((bf16[8,2,64,128]{3,2,1,0:T(8,128)(2,1)}), bf16[8,2,64,128]{3,2,1,0:T(8,128)(2,1)S(1)}, u32[]{:S(2)}, u32[]{:S(2)}) async-start(bf16[8,2,64,128]{3,2,1,0:T(8,128)(2,1)} %bitcast.76), calls=%async_computation.3 | async-start | bytes 524288 | tf_op jit(solution)/shard_map/all_to_all | solution.py:266
  150.6 6.5 %all-to-all-done.3 = bf16[8,2,64,128]{3,2,1,0:T(8,128)(2,1)S(1)} async-done(((bf16[8,2,64,128]{3,2,1,0:T(8,128)(2,1)}), bf16[8,2,64,128]{3,2,1,0:T(8,128)(2,1)S(1)}, u32[]{:S(2)}, u32[]{:S(2)}) %all-to-all-start.3) | async-done | bytes 262176 | tf_op jit(solution)/shard_map/all_to_all | solution.py:266
  158.5 24.8 %all-to-all-start.4 = ((bf16[16,64,128]{2,1,0:T(8,128)(2,1)}), bf16[16,64,128]{2,1,0:T(8,128)(2,1)S(1)}, u32[]{:S(2)}, u32[]{:S(2)}) async-start(bf16[16,64,128]{2,1,0:T(8,128)(2,1)} %bitcast.18), calls=%async_computation.4 | async-start | bytes 524288 | tf_op jit(solution)/shard_map/all_to_all | solution.py:272
  189.0 7.2 %all-to-all-done.4 = bf16[16,64,128]{2,1,0:T(8,128)(2,1)S(1)} async-done(((bf16[16,64,128]{2,1,0:T(8,128)(2,1)}), bf16[16,64,128]{2,1,0:T(8,128)(2,1)S(1)}, u32[]{:S(2)}, u32[]{:S(2)}) %all-to-all-start.4) | async-done | bytes 262176 | tf_op jit(solution)/shard_map/all_to_all | solution.py:272
  197.1 4.0 %all-to-all-start.5 = ((f32[4,64,128]{2,1,0:T(8,128)}), f32[4,64,128]{2,1,0:T(8,128)S(1)}, u32[]{:S(2)}, u32[]{:S(2)}) async-start(f32[4,64,128]{2,1,0:T(8,128)} %broadcast_in_dim.101), calls=%async_computation.5 | async-start | bytes 262144 | tf_op jit(solution)/shard_map/all_to_all | solution.py:204
  201.1 4.8 %all-to-all-done.5 = f32[4,64,128]{2,1,0:T(8,128)S(1)} async-done(((f32[4,64,128]{2,1,0:T(8,128)}), f32[4,64,128]{2,1,0:T(8,128)S(1)}, u32[]{:S(2)}, u32[]{:S(2)}) %all-to-all-start.5) | async-done | bytes 131104 | tf_op jit(solution)/shard_map/all_to_all | solution.py:204
  207.8 28.1 %all_to_all.36 = f32[16,1,128]{2,1,0:T(1,128)S(1)} all-to-all(f32[16,1,128]{2,1,0:T(1,128)S(1)} %broadcast_in_dim_broadcast_in_dim_broadcast_in_dim.3), channel_id=1, replica_groups=mesh['tm'=32,'seq'=16] {'seq'}, dimensions={0} | all-to-all | bytes 16384 | tf_op jit(solution)/shard_map/all_to_all | solution.py:204
  (72 shorter events, 18.6 us)
Async XLA Ops:
  0.6 156.5 %copy-start = (bf16[2560,64]{0,1:T(8,128)(2,1)S(1)}, bf16[2560,64]{0,1:T(8,128)(2,1)}, u32[]{:S(2)}) copy-start(bf16[2560,64]{0,1:T(8,128)(2,1)} %param.25) | copy-start | bytes 983044
  0.6 18.1 %copy-start.3 = (bf16[1,128,2560]{2,1,0:T(8,128)(2,1)S(1)}, bf16[1,128,2560]{2,1,0:T(8,128)(2,1)}, u32[]{:S(2)}) copy-start(bf16[1,128,2560]{2,1,0:T(8,128)(2,1)} %param.16) | copy-start | bytes 1966084
  0.7 62.2 %collective-permute-start.1 = (bf16[128,2560]{1,0:T(8,128)(2,1)}, bf16[128,2560]{1,0:T(8,128)(2,1)S(1)}, u32[]{:S(2)}, u32[]{:S(2)}) collective-permute-start(bf16[128,2560]{1,0:T(8,128)(2,1)} %bitcast.74), channel_id=1, source_target_pairs={{0,2},{1,3},{2,0},{3,1},{4,6},{5,7},{6,4},{7,5},{8,10},{9,11},{10,... | collective-permute-start | bytes 1966088 | tf_op jit(solution)/shard_map/ppermute | solution.py:218
  18.8 37.4 %copy-start.5 = (bf16[2560,128]{1,0:T(8,128)(2,1)S(1)}, bf16[2560,128]{1,0:T(8,128)(2,1)}, u32[]{:S(2)}) copy-start(bf16[2560,128]{1,0:T(8,128)(2,1)} %param.20) | copy-start | bytes 1966084
  18.8 38.4 %copy-start.6 = (bf16[2560,128]{1,0:T(8,128)(2,1)S(1)}, bf16[2560,128]{1,0:T(8,128)(2,1)}, u32[]{:S(2)}) copy-start(bf16[2560,128]{1,0:T(8,128)(2,1)} %param.21) | copy-start | bytes 1966084
  20.5 35.7 %all-to-all-start = ((bf16[4,128,2560]{2,1,0:T(8,128)(2,1)}), bf16[4,128,2560]{2,1,0:T(8,128)(2,1)}, u32[]{:S(2)}, u32[]{:S(2)}) async-start(bf16[4,128,2560]{2,1,0:T(8,128)(2,1)} %broadcast_in_dim.111), calls=%async_computation | async-start | bytes 5242880 | tf_op jit(solution)/shard_map/while/body/all_to_all | solution.py:204
  56.2 2.0 copy-start.7
  59.1 15.1 %collective-permute-start = (bf16[2560,384]{1,0:T(8,128)(2,1)}, bf16[2560,384]{1,0:T(8,128)(2,1)}, u32[]{:S(2)}, u32[]{:S(2)}) collective-permute-start(bf16[2560,384]{1,0:T(8,128)(2,1)} %constant_dynamic-update-slice_fusion.w_mine), channel_id=1, source_target_pairs={{0,1},{1,0},{2,3},{3,2},{4,5},{5,4},{6,7},{7,6},{8,9},{9,8},{10,11... | collective-permute-start | bytes 5898248 | tf_op jit(solution)/shard_map/ppermute | solution.py:226
  64.6 3.8 %copy-start.13 = (s32[32]{0:T(128)S(1)}, s32[32]{0:T(128)}, u32[]{:S(2)}) copy-start(s32[32]{0:T(128)} %param.18) | copy-start | bytes 388
  64.6 5.8 %copy-start.8 = (bf16[2048,64]{0,1:T(8,128)(2,1)S(1)}, bf16[2048,64]{0,1:T(8,128)(2,1)}, u32[]{:S(2)}) copy-start(bf16[2048,64]{0,1:T(8,128)(2,1)} %param.24) | copy-start | bytes 786436
  64.6 35.9 %all-to-all-start.1 = ((bf16[4,128,2560]{2,1,0:T(8,128)(2,1)}), bf16[4,128,2560]{2,1,0:T(8,128)(2,1)S(1)}, u32[]{:S(2)}, u32[]{:S(2)}) async-start(bf16[4,128,2560]{2,1,0:T(8,128)(2,1)} %broadcast_in_dim.91), calls=%async_computation.1 | async-start | bytes 5242880 | tf_op jit(solution)/shard_map/all_to_all | solution.py:204
  82.1 0.9 copy-start.1
  83.0 34.5 %collective-permute-start.2 = (f32[4,128,384]{2,1,0:T(8,128)}, f32[4,128,384]{2,1,0:T(8,128)}, u32[]{:S(2)}, u32[]{:S(2)}) collective-permute-start(f32[4,128,384]{2,1,0:T(8,128)} %get-tuple-element.48), channel_id=1, source_target_pairs={{0,1},{1,0},{2,3},{3,2},{4,5},{5,4},{6,7},{7,6},{8,9},{9,8},{10,11... | collective-permute-start | bytes 2359304 | tf_op jit(solution)/shard_map/ppermute | solution.py:244
  107.7 0.9 copy-start.2
  108.6 21.7 %collective-permute-start.3 = (f32[4,128,384]{2,1,0:T(8,128)}, f32[4,128,384]{2,1,0:T(8,128)S(1)}, u32[]{:S(2)}, u32[]{:S(2)}) collective-permute-start(f32[4,128,384]{2,1,0:T(8,128)} %get-tuple-element.49), channel_id=1, source_target_pairs={{0,1},{1,0},{2,3},{3,2},{4,5},{5,4},{6,7},{7,6},{8,9},{9,8},{10,11... | collective-permute-start | bytes 2359304 | tf_op jit(solution)/shard_map/ppermute | solution.py:244
  111.9 18.3 %all-to-all-start.2 = ((f32[16,16,128]{2,1,0:T(8,128)}), f32[16,16,128]{2,1,0:T(8,128)S(1)}, u32[]{:S(2)}, u32[]{:S(2)}) async-start(f32[16,16,128]{2,1,0:T(8,128)} %broadcast_in_dim.93), calls=%async_computation.2 | async-start | bytes 262144 | tf_op jit(solution)/shard_map/all_to_all | solution.py:204
  130.2 1.0 copy-start.14
  131.2 26.0 %copy-start.4 = (bf16[1,128,2560]{2,1,0:T(8,128)(2,1)S(1)}, bf16[1,128,2560]{2,1,0:T(8,128)(2,1)}, u32[]{:S(2)}) copy-start(bf16[1,128,2560]{2,1,0:T(8,128)(2,1)} %param.16) | copy-start | bytes 1966084
  146.4 39.7 %copy-start.12 = (f32[51]{0:T(128)S(1)}, f32[51]{0:T(128)}, u32[]{:S(2)}) copy-start(f32[51]{0:T(128)} %param.19) | copy-start | bytes 616
  146.4 10.7 %all-to-all-start.3 = ((bf16[8,2,64,128]{3,2,1,0:T(8,128)(2,1)}), bf16[8,2,64,128]{3,2,1,0:T(8,128)(2,1)S(1)}, u32[]{:S(2)}, u32[]{:S(2)}) async-start(bf16[8,2,64,128]{3,2,1,0:T(8,128)(2,1)} %bitcast.76), calls=%async_computation.3 | async-start | bytes 524288 | tf_op jit(solution)/shard_map/all_to_all | solution.py:266
  157.6 48.4 %copy-start.10 = (f32[1,128,64]{1,2,0:T(8,128)S(1)}, f32[1,128,64]{1,2,0:T(8,128)}, u32[]{:S(2)}) copy-start(f32[1,128,64]{1,2,0:T(8,128)} %param.15) | copy-start | bytes 98308
  157.6 48.4 %copy-start.11 = (f32[128,64]{0,1:T(8,128)S(1)}, f32[128,64]{0,1:T(8,128)}, u32[]{:S(2)}) copy-start(f32[128,64]{0,1:T(8,128)} %param.14) | copy-start | bytes 98308
  158.5 37.7 %all-to-all-start.4 = ((bf16[16,64,128]{2,1,0:T(8,128)(2,1)}), bf16[16,64,128]{2,1,0:T(8,128)(2,1)S(1)}, u32[]{:S(2)}, u32[]{:S(2)}) async-start(bf16[16,64,128]{2,1,0:T(8,128)(2,1)} %bitcast.18), calls=%async_computation.4 | async-start | bytes 524288 | tf_op jit(solution)/shard_map/all_to_all | solution.py:272
  197.1 8.8 %all-to-all-start.5 = ((f32[4,64,128]{2,1,0:T(8,128)}), f32[4,64,128]{2,1,0:T(8,128)S(1)}, u32[]{:S(2)}, u32[]{:S(2)}) async-start(f32[4,64,128]{2,1,0:T(8,128)} %broadcast_in_dim.101), calls=%async_computation.5 | async-start | bytes 262144 | tf_op jit(solution)/shard_map/all_to_all | solution.py:204
  (1 other events, 0.7 us)

commit v4 on v3

--- a/solution.py
+++ b/solution.py
@@ -19,6 +19,18 @@
     for x in range(4)
     for y in range(Y)
     for c in range(C)
+]
+
+TO_ACROSS = [(t, t // ZL * ZL + (t + ZL // 2) % ZL) for t in range(4 * ZL)]
+ERROR_GROUPS = [
+    [
+        (x * ZL + (z_lo + z * ZL // 2) % ZL) * Y * Z * C + (y * Z + z) * C + c
+        for z in range(Z)
+        for y in range(Y)
+        for c in range(C)
+    ]
+    for x in range(4)
+    for z_lo in range(ZL)
 ]
 
 
@@ -245,16 +257,14 @@
         powers.append(power)
 
     project_stack(own)
-    for at, rows in enumerate(far):
-        if at > 0:
-            rows, stack = lax.optimization_barrier((rows, stack))
-            project_stack(stack)
-        else:
-            rows, _ = lax.optimization_barrier((rows, own))
-        stack = spread_over(rows, "seq", Y, Y_GROUPS).reshape(-1, raw.shape[1])
-    stack, _ = lax.optimization_barrier((stack, powers))
+    old_here, own_power = lax.optimization_barrier((old_states[0], powers[0]))
+    powers[0] = own_power
+    old_there = lax.ppermute(old_here, "tm", TO_ACROSS)
+    rows, _ = lax.optimization_barrier((far[0], own))
+    stack = spread_over(rows, "seq", Y, Y_GROUPS).reshape(-1, raw.shape[1])
+    stack, old_there = lax.optimization_barrier((stack, old_there))
     project_stack(stack)
-    power_own, power_far = powers[0], jnp.concatenate(powers[1:], axis=2)
+    power_own, power_far = powers
     low = jnp.where(my_z == 0, power_own, power_far)
     high = jnp.where(my_z == 0, power_far, power_own)
     table = jnp.stack([low, high], axis=1).transpose(2, 0, 1, 3).reshape(2 * Y * Z, 128)
@@ -287,11 +297,18 @@
     x_groups = [[x * ZL + z for x in range(4)] for z in range(ZL)]
     totals = spread_over(total, "tm", 4, x_groups)
     before = (jnp.arange(4) < my_x)[:, None, None]
-    earlier = earlier + jnp.sum(jnp.where(before, totals, 0.0), axis=0)
-    new_state = x_start.T + (earlier + increment)
+    entered = jnp.sum(jnp.where(before, totals, 0.0), axis=0) + x_start.T
+    new_state = entered + (earlier + increment)
     change = new_state - old_states[0].T
     square = jnp.sum(change * change)
-    squares = spread_over(jnp.broadcast_to(square, (1, 128)), "seq", Y * Z * C)
+    upto = (jnp.arange(ZL) <= (my_zl + ZL // 2) % ZL)[:, None, None]
+    change_there = entered + jnp.sum(jnp.where(upto, line, 0.0), axis=0) - old_there.T
+    square_there = jnp.sum(change_there * change_there)
+    squares = jnp.where(jnp.arange(Z) == my_z, square, square_there)
+    squares = jnp.broadcast_to(squares[:, None, None, None], (Z, Y * C, 1, 128))
+    squares = lax.all_to_all(
+        squares.reshape(Z * Y * C, 1, 128), ("tm", "seq"), 0, 0, axis_index_groups=ERROR_GROUPS
+    )
     error = (jnp.sum(squares[:, 0, 0]) / (Y * Z * C * change.size)).reshape(1)
     return (drift.T[None], new_state.T[None], error)
 

time: 239 us -> 235 us (0.983)
  starting transfers between devices: 69.6 us -> 79.5 us
  waiting for transfers between devices: 77.8 us -> 68.8 us
  blocking collectives: 28.1 us -> 22.8 us
    all_to_all x4, waiting for transfers between devices: 64.1 us -> 55 us  [spread_over(): return lax.all_to_all(copies, axis, 0, 0, axis_index_groups=groups)]
    ppermute x0 -> x1, starting transfers between devices: none -> 8.02 us  [per_device(): old_there = lax.ppermute(old_here, 'tm', TO_ACROSS)]
    all_to_all x1, blocking collectives: 28.1 us -> 22.8 us  [per_device(): lax.all_to_all(squares.reshape(Z * Y * C, 1, 128), ('tm', 'seq'), 0, 0, a...]
    all_to_all x1, starting transfers between devices: 24.8 us -> 21.5 us  [per_device(): line = lax.all_to_all(sent, ('tm', 'seq'), 0, 0, axis_index_groups=Z_GROUPS)]
    all_to_all x4, starting transfers between devices: 15.9 us -> 19.1 us  [spread_over(): return lax.all_to_all(copies, axis, 0, 0, axis_index_groups=groups)]
    unnamed x33 -> x37, local copies, waits for them, and re-layouts: 5.74 us -> 6.58 us
  transfers between devices with their start and end apart: 10 -> 11, of which waited for: 6 -> 6; matrix products, arithmetic and copies ran while one was open for 7% -> 7% of each run, Pallas kernels for 6% -> 6%
where the time goes in v4:
time: 235 us; the launch traced here: 234 us
  starting transfers between devices  79.5 us (34%)
  waiting for transfers between devices  68.8 us (29%)
  Pallas kernels  29.6 us (13%)
  blocking collectives  22.8 us (10%)
  local copies, waits for them, and re-layouts  17 us (7%)
  between operations  8.65 us (4%)
  other arithmetic  6.97 us (3%)
    all_to_all x4, waiting for transfers between devices, spread_over(): return lax.all_to_all(copies, axis, 0, 0, axis_index_groups=groups)  55 us
    all_to_all x1, blocking collectives, per_device(): lax.all_to_all(squares.reshape(Z * Y * C, 1, 128), ('tm', 'seq'), 0, 0, a...  22.8 us
    all_to_all x1, starting transfers between devices, per_device(): line = lax.all_to_all(sent, ('tm', 'seq'), 0, 0, axis_index_groups=Z_GROUPS)  21.5 us
    all_to_all x4, starting transfers between devices, spread_over(): return lax.all_to_all(copies, axis, 0, 0, axis_index_groups=groups)  19.1 us
    ppermute x1, starting transfers between devices, per_device(): far = [lax.ppermute(raw[a:b], 'seq', TO_FAR) for a, b in CHUNKS]  16.4 us
    pallas_call x1, Pallas kernels, attend(): pl.pallas_call(functools.partial(attend_kernel, chunks), out_shape=jax.Sh...  15.2 us
    pallas_call x2, Pallas kernels, project(): pl.pallas_call(project_kernel, out_shape=(jax.ShapeDtypeStruct((Y, count,...  14.4 us
    ppermute x1, starting transfers between devices, per_device(): old_there = lax.ppermute(old_here, 'tm', TO_ACROSS)  8.02 us
  transfers between devices with their start and end apart: 11, of which 6 were waited for; matrix products, arithmetic and copies ran while one was open for 7% of the time, Pallas kernels for 6%

profile of v4, /device:TPU:1, one launch (start us, length us, event | category | flops | bytes accessed | tf_op | source)
XLA Modules:
  0.0 234.0 jit_solution(445437664709573198)
XLA Ops:
  0.7 16.4 %collective-permute-start.1 = (bf16[128,2560]{1,0:T(8,128)(2,1)}, bf16[128,2560]{1,0:T(8,128)(2,1)S(1)}, u32[]{:S(2)}, u32[]{:S(2)}) collective-permute-start(bf16[128,2560]{1,0:T(8,128)(2,1)} %bitcast.84), channel_id=1, source_target_pairs={{0,2},{1,3},{2,0},{3,1},{4,6},{5,7},{6,4},{7,5},{8,10},{9,11},{10,... | collective-permute-start | bytes 1966088 | tf_op jit(solution)/shard_map/ppermute | solution.py:230
  18.8 37.4 %while.10 = (s32[]{:T(128)}, bf16[4,128,2560]{2,1,0:T(8,128)(2,1)}, s32[]{:T(128)}, bf16[1,128,2560]{2,1,0:T(8,128)(2,1)S(1)}, s32[]{:T(128)}) while((s32[]{:T(128)}, bf16[4,128,2560]{2,1,0:T(8,128)(2,1)}, s32[]{:T(128)}, bf16[1,128,2560]{2,1,0:T(8,128)(2,1)S(1)}, s32[]{:T(128)}) %tuple.45), condition=%wide.region_1.2_spmd, body=%wide.region_0.1_spmd.sunk | while | flops 2 | bytes 11141213 | solution.py:233
  18.8 1.7 broadcast_in_dim.146
  20.5 4.5 %all-to-all-start = ((bf16[4,128,2560]{2,1,0:T(8,128)(2,1)}), bf16[4,128,2560]{2,1,0:T(8,128)(2,1)}, u32[]{:S(2)}, u32[]{:S(2)}) async-start(bf16[4,128,2560]{2,1,0:T(8,128)(2,1)} %broadcast_in_dim.146), calls=%async_computation | async-start | bytes 5242880 | tf_op jit(solution)/shard_map/while/body/all_to_all | solution.py:216
  25.1 31.1 %all-to-all-done = bf16[4,128,2560]{2,1,0:T(8,128)(2,1)} async-done(((bf16[4,128,2560]{2,1,0:T(8,128)(2,1)}), bf16[4,128,2560]{2,1,0:T(8,128)(2,1)}, u32[]{:S(2)}, u32[]{:S(2)}) %all-to-all-start) | async-done | bytes 2621472 | tf_op jit(solution)/shard_map/while/body/all_to_all | solution.py:216
  59.0 3.8 %collective-permute-start = (bf16[2560,384]{1,0:T(8,128)(2,1)}, bf16[2560,384]{1,0:T(8,128)(2,1)}, u32[]{:S(2)}, u32[]{:S(2)}) collective-permute-start(bf16[2560,384]{1,0:T(8,128)(2,1)} %constant_dynamic-update-slice_fusion.w_mine), channel_id=1, source_target_pairs={{0,1},{1,0},{2,3},{3,2},{4,5},{5,4},{6,7},{7,6},{8,9},{9,8},{10,11... | collective-permute-start | bytes 5898248 | tf_op jit(solution)/shard_map/ppermute | solution.py:238
  62.8 1.7 broadcast_in_dim.116
  64.5 3.8 %all-to-all-start.1 = ((bf16[4,128,2560]{2,1,0:T(8,128)(2,1)}), bf16[4,128,2560]{2,1,0:T(8,128)(2,1)S(1)}, u32[]{:S(2)}, u32[]{:S(2)}) async-start(bf16[4,128,2560]{2,1,0:T(8,128)(2,1)} %broadcast_in_dim.116), calls=%async_computation.1 | async-start | bytes 5242880 | tf_op jit(solution)/shard_map/all_to_all | solution.py:216
  71.8 7.2 %project.2 = (f32[4,128,384]{2,1,0:T(8,128)S(1)}, f32[4,128,384]{2,1,0:T(8,128)S(1)}, f32[4,2,128]{2,1,0:T(2,128)S(1)}) custom-call(f32[1,2560]{1,0:T(1,128)S(1)} %get-tuple-element.72.scale_ref, f32[1,2560]{1,0:T(1,128)S(1)} %get-tuple-element.71.shift_ref, bf16[2560,384]{1,0:T(8,128)(2,1)} %constant_dynamic-update-slice_fusion.w_mine, ...), custom_call_target="tpu_custom_call" | custom-call | flops 2013265920 | bytes 6553600 | tf_op jit(solution)/shard_map/project/pallas_call | solution.py:81
  80.9 8.0 %collective-permute-start.2 = (f32[128,64]{0,1:T(8,128)S(1)}, f32[128,64]{0,1:T(8,128)S(1)}, u32[]{:S(2)}, u32[]{:S(2)}) collective-permute-start(f32[128,64]{0,1:T(8,128)S(1)} %bitcast.87), channel_id=1, source_target_pairs={{0,64},{16,80},{32,96},{48,112},{64,0},{80,16},{96,32},{112,48},{1... | collective-permute-start | bytes 98312 | tf_op jit(solution)/shard_map/ppermute | solution.py:262
  90.1 3.9 %collective-permute-start.3 = (f32[4,128,384]{2,1,0:T(8,128)}, f32[4,128,384]{2,1,0:T(8,128)}, u32[]{:S(2)}, u32[]{:S(2)}) collective-permute-start(f32[4,128,384]{2,1,0:T(8,128)} %copy-done.1), channel_id=1, source_target_pairs={{0,1},{1,0},{2,3},{3,2},{4,5},{5,4},{6,7},{7,6},{8,9},{9,8},{10,11... | collective-permute-start | bytes 2359304 | tf_op jit(solution)/shard_map/ppermute | solution.py:256
  94.1 6.3 %all-to-all-done.1 = bf16[4,128,2560]{2,1,0:T(8,128)(2,1)S(1)} async-done(((bf16[4,128,2560]{2,1,0:T(8,128)(2,1)}), bf16[4,128,2560]{2,1,0:T(8,128)(2,1)S(1)}, u32[]{:S(2)}, u32[]{:S(2)}) %all-to-all-start.1) | async-done | bytes 2621472 | tf_op jit(solution)/shard_map/all_to_all | solution.py:216
  100.4 7.2 %project.3 = (f32[4,128,384]{2,1,0:T(8,128)S(1)}, f32[4,128,384]{2,1,0:T(8,128)}, f32[4,2,128]{2,1,0:T(2,128)S(1)}) custom-call(f32[1,2560]{1,0:T(1,128)S(1)} %get-tuple-element.72.scale_ref, f32[1,2560]{1,0:T(1,128)S(1)} %get-tuple-element.71.shift_ref, bf16[2560,384]{1,0:T(8,128)(2,1)} %constant_dynamic-update-slice_fusion.w_mine, ...), custom_call_target="tpu_custom_call" | custom-call | flops 2013265920 | bytes 6553600 | tf_op jit(solution)/shard_map/project/pallas_call | solution.py:81
  108.5 2.7 %collective-permute-start.4 = (f32[4,128,384]{2,1,0:T(8,128)}, f32[4,128,384]{2,1,0:T(8,128)S(1)}, u32[]{:S(2)}, u32[]{:S(2)}) collective-permute-start(f32[4,128,384]{2,1,0:T(8,128)} %get-tuple-element.54), channel_id=1, source_target_pairs={{0,1},{1,0},{2,3},{3,2},{4,5},{5,4},{6,7},{7,6},{8,9},{9,8},{10,11... | collective-permute-start | bytes 2359304 | tf_op jit(solution)/shard_map/ppermute | solution.py:256
  111.9 6.7 %all-to-all-start.2 = ((f32[16,16,128]{2,1,0:T(8,128)}), f32[16,16,128]{2,1,0:T(8,128)S(1)}, u32[]{:S(2)}, u32[]{:S(2)}) async-start(f32[16,16,128]{2,1,0:T(8,128)} %broadcast_in_dim.118), calls=%async_computation.2 | async-start | bytes 262144 | tf_op jit(solution)/shard_map/all_to_all | solution.py:216
  120.7 12.8 %all-to-all-done.2.power_ref = f32[16,16,128]{2,1,0:T(8,128)S(1)} async-done(((f32[16,16,128]{2,1,0:T(8,128)}), f32[16,16,128]{2,1,0:T(8,128)S(1)}, u32[]{:S(2)}, u32[]{:S(2)}) %all-to-all-start.2) | async-done | bytes 131104 | tf_op jit(solution)/shard_map/all_to_all | solution.py:216
  134.4 15.2 %attend.1 = bf16[4,2,2,64,128]{4,3,2,1,0:T(8,128)(2,1)} custom-call(s32[4]{0:T(128)} %pad_add_fusion.place_ref, f32[16,16,128]{2,1,0:T(8,128)} %copy-done.11, f32[2,128]{1,0:T(2,128)} %gain_ref.1, bf16[2048,64]{1,0:T(8,128)(2,1)} %copy.21.w_head_ref, f32[4,128,384]{2,1,0:T(8,128)} %copy-done.2, f32[4,128,384]{2,1,0:T(8,128)} %copy-done.3, ...), custom_call_target="tpu_custom_call" | custom-call | flops 4294967296 | bytes 4194304 | tf_op jit(solution)/shard_map/attend/pallas_call | solution.py:180
  149.6 4.1 %all-to-all-start.3 = ((bf16[8,2,64,128]{3,2,1,0:T(8,128)(2,1)}), bf16[8,2,64,128]{3,2,1,0:T(8,128)(2,1)S(1)}, u32[]{:S(2)}, u32[]{:S(2)}) async-start(bf16[8,2,64,128]{3,2,1,0:T(8,128)(2,1)} %bitcast.86), calls=%async_computation.3 | async-start | bytes 524288 | tf_op jit(solution)/shard_map/all_to_all | solution.py:276
  153.7 6.5 %all-to-all-done.3 = bf16[8,2,64,128]{3,2,1,0:T(8,128)(2,1)S(1)} async-done(((bf16[8,2,64,128]{3,2,1,0:T(8,128)(2,1)}), bf16[8,2,64,128]{3,2,1,0:T(8,128)(2,1)S(1)}, u32[]{:S(2)}, u32[]{:S(2)}) %all-to-all-start.3) | async-done | bytes 262176 | tf_op jit(solution)/shard_map/all_to_all | solution.py:276
  161.6 21.5 %all-to-all-start.4 = ((bf16[16,64,128]{2,1,0:T(8,128)(2,1)}), bf16[16,64,128]{2,1,0:T(8,128)(2,1)S(1)}, u32[]{:S(2)}, u32[]{:S(2)}) async-start(bf16[16,64,128]{2,1,0:T(8,128)(2,1)} %bitcast.19), calls=%async_computation.4 | async-start | bytes 524288 | tf_op jit(solution)/shard_map/all_to_all | solution.py:282
  188.9 7.2 %all-to-all-done.4 = bf16[16,64,128]{2,1,0:T(8,128)(2,1)S(1)} async-done(((bf16[16,64,128]{2,1,0:T(8,128)(2,1)}), bf16[16,64,128]{2,1,0:T(8,128)(2,1)S(1)}, u32[]{:S(2)}, u32[]{:S(2)}) %all-to-all-start.4) | async-done | bytes 262176 | tf_op jit(solution)/shard_map/all_to_all | solution.py:282
  197.0 4.0 %all-to-all-start.5 = ((f32[4,64,128]{2,1,0:T(8,128)}), f32[4,64,128]{2,1,0:T(8,128)S(1)}, u32[]{:S(2)}, u32[]{:S(2)}) async-start(f32[4,64,128]{2,1,0:T(8,128)} %broadcast_in_dim.124), calls=%async_computation.5 | async-start | bytes 262144 | tf_op jit(solution)/shard_map/all_to_all | solution.py:216
  201.0 4.8 %all-to-all-done.5 = f32[4,64,128]{2,1,0:T(8,128)S(1)} async-done(((f32[4,64,128]{2,1,0:T(8,128)}), f32[4,64,128]{2,1,0:T(8,128)S(1)}, u32[]{:S(2)}, u32[]{:S(2)}) %all-to-all-start.5) | async-done | bytes 131104 | tf_op jit(solution)/shard_map/all_to_all | solution.py:216
  208.8 22.8 %all_to_all.36 = f32[16,1,128]{2,1,0:T(1,128)S(1)} all-to-all(f32[16,1,128]{2,1,0:T(1,128)S(1)} %broadcast_in_dim.134), channel_id=1, replica_groups={{0,1,4,5,8,9,12,13,66,67,70,71,74,75,78,79},{16,17,20,21,24,25,28,29,82..., dimensions={0} | all-to-all | bytes 16384 | tf_op jit(solution)/shard_map/all_to_all | solution.py:309
  (81 shorter events, 21.2 us)
Async XLA Ops:
  0.6 159.7 %copy-start = (bf16[2560,64]{0,1:T(8,128)(2,1)S(1)}, bf16[2560,64]{0,1:T(8,128)(2,1)}, u32[]{:S(2)}) copy-start(bf16[2560,64]{0,1:T(8,128)(2,1)} %param.25) | copy-start | bytes 983044
  0.6 18.1 %copy-start.4 = (bf16[1,128,2560]{2,1,0:T(8,128)(2,1)S(1)}, bf16[1,128,2560]{2,1,0:T(8,128)(2,1)}, u32[]{:S(2)}) copy-start(bf16[1,128,2560]{2,1,0:T(8,128)(2,1)} %param.16) | copy-start | bytes 1966084
  0.7 62.2 %collective-permute-start.1 = (bf16[128,2560]{1,0:T(8,128)(2,1)}, bf16[128,2560]{1,0:T(8,128)(2,1)S(1)}, u32[]{:S(2)}, u32[]{:S(2)}) collective-permute-start(bf16[128,2560]{1,0:T(8,128)(2,1)} %bitcast.84), channel_id=1, source_target_pairs={{0,2},{1,3},{2,0},{3,1},{4,6},{5,7},{6,4},{7,5},{8,10},{9,11},{10,... | collective-permute-start | bytes 1966088 | tf_op jit(solution)/shard_map/ppermute | solution.py:230
  18.8 37.4 %copy-start.7 = (bf16[2560,128]{1,0:T(8,128)(2,1)S(1)}, bf16[2560,128]{1,0:T(8,128)(2,1)}, u32[]{:S(2)}) copy-start(bf16[2560,128]{1,0:T(8,128)(2,1)} %param.20) | copy-start | bytes 1966084
  18.8 38.3 %copy-start.8 = (bf16[2560,128]{1,0:T(8,128)(2,1)S(1)}, bf16[2560,128]{1,0:T(8,128)(2,1)}, u32[]{:S(2)}) copy-start(bf16[2560,128]{1,0:T(8,128)(2,1)} %param.21) | copy-start | bytes 1966084
  20.5 35.7 %all-to-all-start = ((bf16[4,128,2560]{2,1,0:T(8,128)(2,1)}), bf16[4,128,2560]{2,1,0:T(8,128)(2,1)}, u32[]{:S(2)}, u32[]{:S(2)}) async-start(bf16[4,128,2560]{2,1,0:T(8,128)(2,1)} %broadcast_in_dim.146), calls=%async_computation | async-start | bytes 5242880 | tf_op jit(solution)/shard_map/while/body/all_to_all | solution.py:216
  56.2 1.9 copy-start.9
  59.0 12.7 %collective-permute-start = (bf16[2560,384]{1,0:T(8,128)(2,1)}, bf16[2560,384]{1,0:T(8,128)(2,1)}, u32[]{:S(2)}, u32[]{:S(2)}) collective-permute-start(bf16[2560,384]{1,0:T(8,128)(2,1)} %constant_dynamic-update-slice_fusion.w_mine), channel_id=1, source_target_pairs={{0,1},{1,0},{2,3},{3,2},{4,5},{5,4},{6,7},{7,6},{8,9},{9,8},{10,11... | collective-permute-start | bytes 5898248 | tf_op jit(solution)/shard_map/ppermute | solution.py:238
  64.5 3.8 %copy-start.15 = (s32[32]{0:T(128)S(1)}, s32[32]{0:T(128)}, u32[]{:S(2)}) copy-start(s32[32]{0:T(128)} %param.18) | copy-start | bytes 388
  64.5 35.9 %all-to-all-start.1 = ((bf16[4,128,2560]{2,1,0:T(8,128)(2,1)}), bf16[4,128,2560]{2,1,0:T(8,128)(2,1)S(1)}, u32[]{:S(2)}, u32[]{:S(2)}) async-start(bf16[4,128,2560]{2,1,0:T(8,128)(2,1)} %broadcast_in_dim.116), calls=%async_computation.1 | async-start | bytes 5242880 | tf_op jit(solution)/shard_map/all_to_all | solution.py:216
  71.8 9.1 %copy-start.12 = (f32[1,128,64]{1,2,0:T(8,128)S(1)}, f32[1,128,64]{1,2,0:T(8,128)}, u32[]{:S(2)}) copy-start(f32[1,128,64]{1,2,0:T(8,128)} %param.15) | copy-start | bytes 98308
  71.8 17.1 %copy-start.5 = (bf16[1,128,2560]{2,1,0:T(8,128)(2,1)S(1)}, bf16[1,128,2560]{2,1,0:T(8,128)(2,1)}, u32[]{:S(2)}) copy-start(bf16[1,128,2560]{2,1,0:T(8,128)(2,1)} %param.16) | copy-start | bytes 1966084
  71.8 17.3 %copy-start.10 = (bf16[2048,64]{0,1:T(8,128)(2,1)S(1)}, bf16[2048,64]{0,1:T(8,128)(2,1)}, u32[]{:S(2)}) copy-start(bf16[2048,64]{0,1:T(8,128)(2,1)} %param.24) | copy-start | bytes 786436
  80.9 13.2 %collective-permute-start.2 = (f32[128,64]{0,1:T(8,128)S(1)}, f32[128,64]{0,1:T(8,128)S(1)}, u32[]{:S(2)}, u32[]{:S(2)}) collective-permute-start(f32[128,64]{0,1:T(8,128)S(1)} %bitcast.87), channel_id=1, source_target_pairs={{0,64},{16,80},{32,96},{48,112},{64,0},{80,16},{96,32},{112,48},{1... | collective-permute-start | bytes 98312 | tf_op jit(solution)/shard_map/ppermute | solution.py:262
  90.1 30.5 %collective-permute-start.3 = (f32[4,128,384]{2,1,0:T(8,128)}, f32[4,128,384]{2,1,0:T(8,128)}, u32[]{:S(2)}, u32[]{:S(2)}) collective-permute-start(f32[4,128,384]{2,1,0:T(8,128)} %copy-done.1), channel_id=1, source_target_pairs={{0,1},{1,0},{2,3},{3,2},{4,5},{5,4},{6,7},{7,6},{8,9},{9,8},{10,11... | collective-permute-start | bytes 2359304 | tf_op jit(solution)/shard_map/ppermute | solution.py:256
  108.5 25.0 %collective-permute-start.4 = (f32[4,128,384]{2,1,0:T(8,128)}, f32[4,128,384]{2,1,0:T(8,128)S(1)}, u32[]{:S(2)}, u32[]{:S(2)}) collective-permute-start(f32[4,128,384]{2,1,0:T(8,128)} %get-tuple-element.54), channel_id=1, source_target_pairs={{0,1},{1,0},{2,3},{3,2},{4,5},{5,4},{6,7},{7,6},{8,9},{9,8},{10,11... | collective-permute-start | bytes 2359304 | tf_op jit(solution)/shard_map/ppermute | solution.py:256
  111.9 21.6 %all-to-all-start.2 = ((f32[16,16,128]{2,1,0:T(8,128)}), f32[16,16,128]{2,1,0:T(8,128)S(1)}, u32[]{:S(2)}, u32[]{:S(2)}) async-start(f32[16,16,128]{2,1,0:T(8,128)} %broadcast_in_dim.118), calls=%async_computation.2 | async-start | bytes 262144 | tf_op jit(solution)/shard_map/all_to_all | solution.py:216
  133.4 0.9 copy-start.16
  134.4 25.9 %copy-start.6 = (bf16[1,128,2560]{2,1,0:T(8,128)(2,1)S(1)}, bf16[1,128,2560]{2,1,0:T(8,128)(2,1)}, u32[]{:S(2)}) copy-start(bf16[1,128,2560]{2,1,0:T(8,128)(2,1)} %param.16) | copy-start | bytes 1966084
  149.6 36.3 %copy-start.14 = (f32[51]{0:T(128)S(1)}, f32[51]{0:T(128)}, u32[]{:S(2)}) copy-start(f32[51]{0:T(128)} %param.19) | copy-start | bytes 616
  149.6 10.6 %all-to-all-start.3 = ((bf16[8,2,64,128]{3,2,1,0:T(8,128)(2,1)}), bf16[8,2,64,128]{3,2,1,0:T(8,128)(2,1)S(1)}, u32[]{:S(2)}, u32[]{:S(2)}) async-start(bf16[8,2,64,128]{3,2,1,0:T(8,128)(2,1)} %bitcast.86), calls=%async_computation.3 | async-start | bytes 524288 | tf_op jit(solution)/shard_map/all_to_all | solution.py:276
  160.8 45.1 %copy-start.13 = (f32[128,64]{0,1:T(8,128)S(1)}, f32[128,64]{0,1:T(8,128)}, u32[]{:S(2)}) copy-start(f32[128,64]{0,1:T(8,128)} %param.14) | copy-start | bytes 98308
  161.6 34.5 %all-to-all-start.4 = ((bf16[16,64,128]{2,1,0:T(8,128)(2,1)}), bf16[16,64,128]{2,1,0:T(8,128)(2,1)S(1)}, u32[]{:S(2)}, u32[]{:S(2)}) async-start(bf16[16,64,128]{2,1,0:T(8,128)(2,1)} %bitcast.19), calls=%async_computation.4 | async-start | bytes 524288 | tf_op jit(solution)/shard_map/all_to_all | solution.py:282
  197.0 8.8 %all-to-all-start.5 = ((f32[4,64,128]{2,1,0:T(8,128)}), f32[4,64,128]{2,1,0:T(8,128)S(1)}, u32[]{:S(2)}, u32[]{:S(2)}) async-start(f32[4,64,128]{2,1,0:T(8,128)} %broadcast_in_dim.124), calls=%async_computation.5 | async-start | bytes 262144 | tf_op jit(solution)/shard_map/all_to_all | solution.py:216
  (4 other events, 3.3 us)

commit v5 on v4

--- a/solution.py
+++ b/solution.py
@@ -50,9 +50,9 @@
 TO_FAR = seq_perm(lambda y, z, c: (y, 1 - z, c))
 
 
-def project_kernel(
-    scale_ref, shift_ref, w_mine, w_theirs, rows_ref, mine_ref, other_ref, power_ref, normed_ref
-):
+def project_kernel(scale_ref, shift_ref, w_mine, w_theirs, rows_ref, *refs):
+    power_ref, normed_ref = refs[-2:]
+    mine_refs, other_refs = refs[: len(refs) // 2 - 1], refs[len(refs) // 2 - 1 : -2]
     rows = rows_ref[...].astype(jnp.float32)
     average = jnp.mean(rows, axis=-1, keepdims=True)
     centred = rows - average
@@ -64,8 +64,10 @@
     count = mine.shape[0] // Y
     for y in range(Y):
         rows = slice(y * count, (y + 1) * count)
-        mine_ref[y] = mine[rows]
-        other_ref[y] = other[rows]
+        for outs, wide in ((mine_refs, mine), (other_refs, other)):
+            size = count // len(outs)
+            for at, out in enumerate(outs):
+                out[y] = wide[y * count + at * size : y * count + (at + 1) * size]
         for part in range(2):
             cols = slice(part * 128, (part + 1) * 128)
             squares = mine[rows, cols] * mine[rows, cols] + other[rows, cols] * other[rows, cols]
@@ -74,19 +76,16 @@
             )
 
 
-def project(scale, shift, w_mine, w_theirs, rows):
+def project(scale, shift, w_mine, w_theirs, rows, cuts):
     features, columns = w_mine.shape
     count = rows.shape[0] // Y
     vmem = pl.BlockSpec(memory_space=pltpu.VMEM)
-    return pl.pallas_call(
+    stack = jax.ShapeDtypeStruct((Y, count // cuts, columns), jnp.float32)
+    outs = pl.pallas_call(
         project_kernel,
-        out_shape=(
-            jax.ShapeDtypeStruct((Y, count, columns), jnp.float32),
-            jax.ShapeDtypeStruct((Y, count, columns), jnp.float32),
-            jax.ShapeDtypeStruct((Y, 2, count), jnp.float32),
-        ),
+        out_shape=(stack,) * (2 * cuts) + (jax.ShapeDtypeStruct((Y, 2, count), jnp.float32),),
         in_specs=[vmem] * 5,
-        out_specs=(vmem, vmem, vmem),
+        out_specs=(vmem,) * (2 * cuts + 1),
         scratch_shapes=[pltpu.VMEM(rows.shape, jnp.bfloat16)],
         compiler_params=pltpu.CompilerParams(vmem_limit_bytes=24 * 2**20),
         cost_estimate=pl.CostEstimate(
@@ -96,6 +95,7 @@
         ),
         name="project",
     )(scale, shift, w_mine, w_theirs, rows)
+    return outs[:cuts], outs[cuts : 2 * cuts], outs[-1]
 
 
 def attend_kernel(chunks, place_ref, power_ref, gain_ref, w_head_ref, *refs):
@@ -250,27 +250,27 @@
 
     mine, theirs, powers = [], [], []
 
-    def project_stack(rows):
-        kept, given, power = project(scale, shift, w_mine, w_theirs, rows)
-        mine.append(kept)
-        theirs.append(lax.ppermute(given, "seq", TO_CORE))
+    def project_stack(rows, cuts):
+        kept, given, power = project(scale, shift, w_mine, w_theirs, rows, cuts)
+        mine.extend(kept)
+        theirs.extend(lax.ppermute(part, "seq", TO_CORE) for part in given)
         powers.append(power)
 
-    project_stack(own)
+    project_stack(own, 1)
     old_here, own_power = lax.optimization_barrier((old_states[0], powers[0]))
     powers[0] = own_power
     old_there = lax.ppermute(old_here, "tm", TO_ACROSS)
     rows, _ = lax.optimization_barrier((far[0], own))
     stack = spread_over(rows, "seq", Y, Y_GROUPS).reshape(-1, raw.shape[1])
     stack, old_there = lax.optimization_barrier((stack, old_there))
-    project_stack(stack)
+    project_stack(stack, 2)
     power_own, power_far = powers
     low = jnp.where(my_z == 0, power_own, power_far)
     high = jnp.where(my_z == 0, power_far, power_own)
     table = jnp.stack([low, high], axis=1).transpose(2, 0, 1, 3).reshape(2 * Y * Z, 128)
     powers = spread_over(table, "seq", Y * Z * C)
 
-    chunks = ((0, 0, 128),) + tuple((1, a, b) for a, b in CHUNKS)
+    chunks = ((0, 0, 128),) + ((1, 0, 64), (1, 64, 128))
     partial = attend(chunks, place, powers, qk_gain, w_head, mine, theirs)
     partial = partial.reshape(Y * C, Z, LAT, 128)
     partial = lax.all_to_all(partial, "seq", 0, 0, axis_index_groups=YC_GROUPS)

time: 235 us -> 235 us (level)
  waiting for transfers between devices: 68.8 us -> 63.3 us
  starting transfers between devices: 79.5 us -> 83.2 us
    all_to_all x4, waiting for transfers between devices: 55 us -> 49.6 us  [spread_over(): return lax.all_to_all(copies, axis, 0, 0, axis_index_groups=groups)]
    all_to_all x1, starting transfers between devices: 21.5 us -> 24.2 us  [per_device(): line = lax.all_to_all(sent, ('tm', 'seq'), 0, 0, axis_index_groups=Z_GROUPS)]
    unnamed x37 -> x41, local copies, waits for them, and re-layouts: 6.58 us -> 8.63 us
    ppermute x2 -> x3, starting transfers between devices: 6.62 us -> 8.44 us  [project_stack(): theirs.extend((lax.ppermute(part, 'seq', TO_CORE) for part in given))]
  transfers between devices with their start and end apart: 11 -> 12, of which waited for: 6 -> 6; matrix products, arithmetic and copies ran while one was open for 7% -> 7% of each run, Pallas kernels for 6% -> 6%
where the time goes in v5:
time: 235 us; the launch traced here: 234 us
  starting transfers between devices  83.2 us (35%)
  waiting for transfers between devices  63.3 us (27%)
  Pallas kernels  28.8 us (12%)
  blocking collectives  22.8 us (10%)
  local copies, waits for them, and re-layouts  19 us (8%)
  between operations  8.68 us (4%)
  other arithmetic  7.01 us (3%)
    all_to_all x4, waiting for transfers between devices, spread_over(): return lax.all_to_all(copies, axis, 0, 0, axis_index_groups=groups)  49.6 us
    all_to_all x1, starting transfers between devices, per_device(): line = lax.all_to_all(sent, ('tm', 'seq'), 0, 0, axis_index_groups=Z_GROUPS)  24.2 us
    all_to_all x1, blocking collectives, per_device(): lax.all_to_all(squares.reshape(Z * Y * C, 1, 128), ('tm', 'seq'), 0, 0, a...  22.8 us
    all_to_all x4, starting transfers between devices, spread_over(): return lax.all_to_all(copies, axis, 0, 0, axis_index_groups=groups)  18.4 us
    ppermute x1, starting transfers between devices, per_device(): far = [lax.ppermute(raw[a:b], 'seq', TO_FAR) for a, b in CHUNKS]  16.4 us
    pallas_call x1, Pallas kernels, attend(): pl.pallas_call(functools.partial(attend_kernel, chunks), out_shape=jax.Sh...  15.2 us
    pallas_call x2, Pallas kernels, project(): pl.pallas_call(project_kernel, out_shape=(stack,) * (2 * cuts) + (jax.Sha...  13.6 us
    unnamed x41, local copies, waits for them, and re-layouts  8.63 us
  transfers between devices with their start and end apart: 12, of which 6 were waited for; matrix products, arithmetic and copies ran while one was open for 7% of the time, Pallas kernels for 6%

profile of v5, /device:TPU:1, one launch (start us, length us, event | category | flops | bytes accessed | tf_op | source)
XLA Modules:
  0.0 233.6 jit_solution(4383887355443215845)
XLA Ops:
  0.7 16.4 %collective-permute-start.1 = (bf16[128,2560]{1,0:T(8,128)(2,1)}, bf16[128,2560]{1,0:T(8,128)(2,1)S(1)}, u32[]{:S(2)}, u32[]{:S(2)}) collective-permute-start(bf16[128,2560]{1,0:T(8,128)(2,1)} %bitcast.84), channel_id=1, source_target_pairs={{0,2},{1,3},{2,0},{3,1},{4,6},{5,7},{6,4},{7,5},{8,10},{9,11},{10,... | collective-permute-start | bytes 1966088 | tf_op jit(solution)/shard_map/ppermute | solution.py:230
  18.8 37.4 %while.10 = (s32[]{:T(128)}, bf16[4,128,2560]{2,1,0:T(8,128)(2,1)}, s32[]{:T(128)}, bf16[1,128,2560]{2,1,0:T(8,128)(2,1)S(1)}, s32[]{:T(128)}) while((s32[]{:T(128)}, bf16[4,128,2560]{2,1,0:T(8,128)(2,1)}, s32[]{:T(128)}, bf16[1,128,2560]{2,1,0:T(8,128)(2,1)S(1)}, s32[]{:T(128)}) %tuple.45), condition=%wide.region_1.2_spmd, body=%wide.region_0.1_spmd.sunk | while | flops 2 | bytes 11141213 | solution.py:233
  20.5 4.6 %all-to-all-start = ((bf16[4,128,2560]{2,1,0:T(8,128)(2,1)}), bf16[4,128,2560]{2,1,0:T(8,128)(2,1)}, u32[]{:S(2)}, u32[]{:S(2)}) async-start(bf16[4,128,2560]{2,1,0:T(8,128)(2,1)} %broadcast_in_dim.146), calls=%async_computation | async-start | bytes 5242880 | tf_op jit(solution)/shard_map/while/body/all_to_all | solution.py:216
  25.1 31.1 %all-to-all-done = bf16[4,128,2560]{2,1,0:T(8,128)(2,1)} async-done(((bf16[4,128,2560]{2,1,0:T(8,128)(2,1)}), bf16[4,128,2560]{2,1,0:T(8,128)(2,1)}, u32[]{:S(2)}, u32[]{:S(2)}) %all-to-all-start) | async-done | bytes 2621472 | tf_op jit(solution)/shard_map/while/body/all_to_all | solution.py:216
  59.1 3.8 %collective-permute-start = (bf16[2560,384]{1,0:T(8,128)(2,1)}, bf16[2560,384]{1,0:T(8,128)(2,1)}, u32[]{:S(2)}, u32[]{:S(2)}) collective-permute-start(bf16[2560,384]{1,0:T(8,128)(2,1)} %constant_dynamic-update-slice_fusion.w_mine), channel_id=1, source_target_pairs={{0,1},{1,0},{2,3},{3,2},{4,5},{5,4},{6,7},{7,6},{8,9},{9,8},{10,11... | collective-permute-start | bytes 5898248 | tf_op jit(solution)/shard_map/ppermute | solution.py:238
  64.6 3.8 %all-to-all-start.1 = ((bf16[4,128,2560]{2,1,0:T(8,128)(2,1)}), bf16[4,128,2560]{2,1,0:T(8,128)(2,1)S(1)}, u32[]{:S(2)}, u32[]{:S(2)}) async-start(bf16[4,128,2560]{2,1,0:T(8,128)(2,1)} %broadcast_in_dim.116), calls=%async_computation.1 | async-start | bytes 5242880 | tf_op jit(solution)/shard_map/all_to_all | solution.py:216
  71.8 7.2 %project.2 = (f32[4,128,384]{2,1,0:T(8,128)S(1)}, f32[4,128,384]{2,1,0:T(8,128)S(1)}, f32[4,2,128]{2,1,0:T(2,128)S(1)}) custom-call(f32[1,2560]{1,0:T(1,128)S(1)} %get-tuple-element.76.scale_ref, f32[1,2560]{1,0:T(1,128)S(1)} %get-tuple-element.75.shift_ref, bf16[2560,384]{1,0:T(8,128)(2,1)} %constant_dynamic-update-slice_fusion.w_mine, ...), custom_call_target="tpu_custom_call" | custom-call | flops 2013265920 | bytes 6553600 | tf_op jit(solution)/shard_map/project/pallas_call | solution.py:84
  80.9 8.0 %collective-permute-start.2 = (f32[128,64]{0,1:T(8,128)S(1)}, f32[128,64]{0,1:T(8,128)S(1)}, u32[]{:S(2)}, u32[]{:S(2)}) collective-permute-start(f32[128,64]{0,1:T(8,128)S(1)} %bitcast.87), channel_id=1, source_target_pairs={{0,64},{16,80},{32,96},{48,112},{64,0},{80,16},{96,32},{112,48},{1... | collective-permute-start | bytes 98312 | tf_op jit(solution)/shard_map/ppermute | solution.py:262
  89.1 3.9 %collective-permute-start.3 = (f32[4,128,384]{2,1,0:T(8,128)}, f32[4,128,384]{2,1,0:T(8,128)}, u32[]{:S(2)}, u32[]{:S(2)}) collective-permute-start(f32[4,128,384]{2,1,0:T(8,128)} %copy-done.1), channel_id=1, source_target_pairs={{0,1},{1,0},{2,3},{3,2},{4,5},{5,4},{6,7},{7,6},{8,9},{9,8},{10,11... | collective-permute-start | bytes 2359304 | tf_op jit(solution)/shard_map/ppermute | solution.py:256
  93.0 7.4 %all-to-all-done.1 = bf16[4,128,2560]{2,1,0:T(8,128)(2,1)S(1)} async-done(((bf16[4,128,2560]{2,1,0:T(8,128)(2,1)}), bf16[4,128,2560]{2,1,0:T(8,128)(2,1)S(1)}, u32[]{:S(2)}, u32[]{:S(2)}) %all-to-all-start.1) | async-done | bytes 2621472 | tf_op jit(solution)/shard_map/all_to_all | solution.py:216
  100.4 6.4 %project.3 = (f32[4,64,384]{2,1,0:T(8,128)S(1)}, f32[4,64,384]{2,1,0:T(8,128)S(1)}, f32[4,64,384]{2,1,0:T(8,128)S(1)}, f32[4,64,384]{2,1,0:T(8,128)S(1)}, f32[4,2,128]{2,1,0:T(2,128)S(1)}) custom-call(f32[1,2560]{1,0:T(1,128)S(1)} %get-tuple-element.76.scale_ref, f32[1,2560]{1,0:T(1,128)S(1)} %get-tuple-element.75.shift_ref, ...), custom_call_target="tpu_custom_call" | custom-call | flops 2013265920 | bytes 6553600 | tf_op jit(solution)/shard_map/project/pallas_call | solution.py:84
  109.8 6.0 %all-to-all-start.2 = ((f32[16,16,128]{2,1,0:T(8,128)}), f32[16,16,128]{2,1,0:T(8,128)S(1)}, u32[]{:S(2)}, u32[]{:S(2)}) async-start(f32[16,16,128]{2,1,0:T(8,128)} %broadcast_in_dim.118), calls=%async_computation.2 | async-start | bytes 262144 | tf_op jit(solution)/shard_map/all_to_all | solution.py:216
  115.8 2.0 collective-permute-start.4
  117.8 2.5 %collective-permute-start.5 = (f32[4,64,384]{2,1,0:T(8,128)S(1)}, f32[4,64,384]{2,1,0:T(8,128)S(1)}, u32[]{:S(2)}, u32[]{:S(2)}) collective-permute-start(f32[4,64,384]{2,1,0:T(8,128)S(1)} %get-tuple-element.58), channel_id=1, source_target_pairs={{0,1},{1,0},{2,3},{3,2},{4,5},{5,4},{6,7},{7,6},{8,9},{9,8},{10,11... | collective-permute-start | bytes 1179656 | tf_op jit(solution)/shard_map/ppermute | solution.py:256
  121.0 2.0 copy.21.w_head_ref
  124.4 6.3 %all-to-all-done.2.power_ref = f32[16,16,128]{2,1,0:T(8,128)S(1)} async-done(((f32[16,16,128]{2,1,0:T(8,128)}), f32[16,16,128]{2,1,0:T(8,128)S(1)}, u32[]{:S(2)}, u32[]{:S(2)}) %all-to-all-start.2) | async-done | bytes 131104 | tf_op jit(solution)/shard_map/all_to_all | solution.py:216
  131.3 15.2 %attend.1 = bf16[4,2,2,64,128]{4,3,2,1,0:T(8,128)(2,1)} custom-call(s32[4]{0:T(128)} %pad_add_fusion.place_ref, f32[16,16,128]{2,1,0:T(8,128)} %copy-done.12, f32[2,128]{1,0:T(2,128)} %gain_ref.1, bf16[2048,64]{1,0:T(8,128)(2,1)} %copy.21.w_head_ref, f32[4,128,384]{2,1,0:T(8,128)} %copy-done.3, f32[4,64,384]{2,1,0:T(8,128)} %copy-done.4, ...), custom_call_target="tpu_custom_call" | custom-call | flops 4294967296 | bytes 4194304 | tf_op jit(solution)/shard_map/attend/pallas_call | solution.py:180
  146.6 4.1 %all-to-all-start.3 = ((bf16[8,2,64,128]{3,2,1,0:T(8,128)(2,1)}), bf16[8,2,64,128]{3,2,1,0:T(8,128)(2,1)S(1)}, u32[]{:S(2)}, u32[]{:S(2)}) async-start(bf16[8,2,64,128]{3,2,1,0:T(8,128)(2,1)} %bitcast.86), calls=%async_computation.3 | async-start | bytes 524288 | tf_op jit(solution)/shard_map/all_to_all | solution.py:276
  150.7 6.5 %all-to-all-done.3 = bf16[8,2,64,128]{3,2,1,0:T(8,128)(2,1)S(1)} async-done(((bf16[8,2,64,128]{3,2,1,0:T(8,128)(2,1)}), bf16[8,2,64,128]{3,2,1,0:T(8,128)(2,1)S(1)}, u32[]{:S(2)}, u32[]{:S(2)}) %all-to-all-start.3) | async-done | bytes 262176 | tf_op jit(solution)/shard_map/all_to_all | solution.py:276
  158.6 24.2 %all-to-all-start.4 = ((bf16[16,64,128]{2,1,0:T(8,128)(2,1)}), bf16[16,64,128]{2,1,0:T(8,128)(2,1)S(1)}, u32[]{:S(2)}, u32[]{:S(2)}) async-start(bf16[16,64,128]{2,1,0:T(8,128)(2,1)} %bitcast.19), calls=%async_computation.4 | async-start | bytes 524288 | tf_op jit(solution)/shard_map/all_to_all | solution.py:282
  188.5 7.2 %all-to-all-done.4 = bf16[16,64,128]{2,1,0:T(8,128)(2,1)S(1)} async-done(((bf16[16,64,128]{2,1,0:T(8,128)(2,1)}), bf16[16,64,128]{2,1,0:T(8,128)(2,1)S(1)}, u32[]{:S(2)}, u32[]{:S(2)}) %all-to-all-start.4) | async-done | bytes 262176 | tf_op jit(solution)/shard_map/all_to_all | solution.py:282
  196.6 4.0 %all-to-all-start.5 = ((f32[4,64,128]{2,1,0:T(8,128)}), f32[4,64,128]{2,1,0:T(8,128)S(1)}, u32[]{:S(2)}, u32[]{:S(2)}) async-start(f32[4,64,128]{2,1,0:T(8,128)} %broadcast_in_dim.124), calls=%async_computation.5 | async-start | bytes 262144 | tf_op jit(solution)/shard_map/all_to_all | solution.py:216
  200.6 4.8 %all-to-all-done.5 = f32[4,64,128]{2,1,0:T(8,128)S(1)} async-done(((f32[4,64,128]{2,1,0:T(8,128)}), f32[4,64,128]{2,1,0:T(8,128)S(1)}, u32[]{:S(2)}, u32[]{:S(2)}) %all-to-all-start.5) | async-done | bytes 131104 | tf_op jit(solution)/shard_map/all_to_all | solution.py:216
  208.4 22.8 %all_to_all.36 = f32[16,1,128]{2,1,0:T(1,128)S(1)} all-to-all(f32[16,1,128]{2,1,0:T(1,128)S(1)} %broadcast_in_dim.134), channel_id=1, replica_groups={{0,1,4,5,8,9,12,13,66,67,70,71,74,75,78,79},{16,17,20,21,24,25,28,29,82..., dimensions={0} | all-to-all | bytes 16384 | tf_op jit(solution)/shard_map/all_to_all | solution.py:309
  (87 shorter events, 24.7 us)
Async XLA Ops:
  0.6 156.6 %copy-start = (bf16[2560,64]{0,1:T(8,128)(2,1)S(1)}, bf16[2560,64]{0,1:T(8,128)(2,1)}, u32[]{:S(2)}) copy-start(bf16[2560,64]{0,1:T(8,128)(2,1)} %param.25) | copy-start | bytes 983044
  0.6 18.1 %copy-start.6 = (bf16[1,128,2560]{2,1,0:T(8,128)(2,1)S(1)}, bf16[1,128,2560]{2,1,0:T(8,128)(2,1)}, u32[]{:S(2)}) copy-start(bf16[1,128,2560]{2,1,0:T(8,128)(2,1)} %param.16) | copy-start | bytes 1966084
  0.7 62.2 %collective-permute-start.1 = (bf16[128,2560]{1,0:T(8,128)(2,1)}, bf16[128,2560]{1,0:T(8,128)(2,1)S(1)}, u32[]{:S(2)}, u32[]{:S(2)}) collective-permute-start(bf16[128,2560]{1,0:T(8,128)(2,1)} %bitcast.84), channel_id=1, source_target_pairs={{0,2},{1,3},{2,0},{3,1},{4,6},{5,7},{6,4},{7,5},{8,10},{9,11},{10,... | collective-permute-start | bytes 1966088 | tf_op jit(solution)/shard_map/ppermute | solution.py:230
  18.8 37.4 %copy-start.9 = (bf16[2560,128]{1,0:T(8,128)(2,1)S(1)}, bf16[2560,128]{1,0:T(8,128)(2,1)}, u32[]{:S(2)}) copy-start(bf16[2560,128]{1,0:T(8,128)(2,1)} %param.20) | copy-start | bytes 1966084
  18.8 38.3 %copy-start.10 = (bf16[2560,128]{1,0:T(8,128)(2,1)S(1)}, bf16[2560,128]{1,0:T(8,128)(2,1)}, u32[]{:S(2)}) copy-start(bf16[2560,128]{1,0:T(8,128)(2,1)} %param.21) | copy-start | bytes 1966084
  20.5 35.7 %all-to-all-start = ((bf16[4,128,2560]{2,1,0:T(8,128)(2,1)}), bf16[4,128,2560]{2,1,0:T(8,128)(2,1)}, u32[]{:S(2)}, u32[]{:S(2)}) async-start(bf16[4,128,2560]{2,1,0:T(8,128)(2,1)} %broadcast_in_dim.146), calls=%async_computation | async-start | bytes 5242880 | tf_op jit(solution)/shard_map/while/body/all_to_all | solution.py:216
  59.1 12.7 %collective-permute-start = (bf16[2560,384]{1,0:T(8,128)(2,1)}, bf16[2560,384]{1,0:T(8,128)(2,1)}, u32[]{:S(2)}, u32[]{:S(2)}) collective-permute-start(bf16[2560,384]{1,0:T(8,128)(2,1)} %constant_dynamic-update-slice_fusion.w_mine), channel_id=1, source_target_pairs={{0,1},{1,0},{2,3},{3,2},{4,5},{5,4},{6,7},{7,6},{8,9},{9,8},{10,11... | collective-permute-start | bytes 5898248 | tf_op jit(solution)/shard_map/ppermute | solution.py:238
  64.6 3.8 %copy-start.16 = (s32[32]{0:T(128)S(1)}, s32[32]{0:T(128)}, u32[]{:S(2)}) copy-start(s32[32]{0:T(128)} %param.18) | copy-start | bytes 388
  64.6 35.9 %all-to-all-start.1 = ((bf16[4,128,2560]{2,1,0:T(8,128)(2,1)}), bf16[4,128,2560]{2,1,0:T(8,128)(2,1)S(1)}, u32[]{:S(2)}, u32[]{:S(2)}) async-start(bf16[4,128,2560]{2,1,0:T(8,128)(2,1)} %broadcast_in_dim.116), calls=%async_computation.1 | async-start | bytes 5242880 | tf_op jit(solution)/shard_map/all_to_all | solution.py:216
  71.8 9.0 %copy-start.13 = (f32[1,128,64]{1,2,0:T(8,128)S(1)}, f32[1,128,64]{1,2,0:T(8,128)}, u32[]{:S(2)}) copy-start(f32[1,128,64]{1,2,0:T(8,128)} %param.15) | copy-start | bytes 98308
  71.8 17.0 %copy-start.7 = (bf16[1,128,2560]{2,1,0:T(8,128)(2,1)S(1)}, bf16[1,128,2560]{2,1,0:T(8,128)(2,1)}, u32[]{:S(2)}) copy-start(bf16[1,128,2560]{2,1,0:T(8,128)(2,1)} %param.16) | copy-start | bytes 1966084
  80.9 12.2 %collective-permute-start.2 = (f32[128,64]{0,1:T(8,128)S(1)}, f32[128,64]{0,1:T(8,128)S(1)}, u32[]{:S(2)}, u32[]{:S(2)}) collective-permute-start(f32[128,64]{0,1:T(8,128)S(1)} %bitcast.87), channel_id=1, source_target_pairs={{0,64},{16,80},{32,96},{48,112},{64,0},{80,16},{96,32},{112,48},{1... | collective-permute-start | bytes 98312 | tf_op jit(solution)/shard_map/ppermute | solution.py:262
  89.1 35.2 %collective-permute-start.3 = (f32[4,128,384]{2,1,0:T(8,128)}, f32[4,128,384]{2,1,0:T(8,128)}, u32[]{:S(2)}, u32[]{:S(2)}) collective-permute-start(f32[4,128,384]{2,1,0:T(8,128)} %copy-done.1), channel_id=1, source_target_pairs={{0,1},{1,0},{2,3},{3,2},{4,5},{5,4},{6,7},{7,6},{8,9},{9,8},{10,11... | collective-permute-start | bytes 2359304 | tf_op jit(solution)/shard_map/ppermute | solution.py:256
  109.8 20.9 %all-to-all-start.2 = ((f32[16,16,128]{2,1,0:T(8,128)}), f32[16,16,128]{2,1,0:T(8,128)S(1)}, u32[]{:S(2)}, u32[]{:S(2)}) async-start(f32[16,16,128]{2,1,0:T(8,128)} %broadcast_in_dim.118), calls=%async_computation.2 | async-start | bytes 262144 | tf_op jit(solution)/shard_map/all_to_all | solution.py:216
  115.8 8.5 %collective-permute-start.4 = (f32[4,64,384]{2,1,0:T(8,128)}, f32[4,64,384]{2,1,0:T(8,128)S(1)}, u32[]{:S(2)}, u32[]{:S(2)}) collective-permute-start(f32[4,64,384]{2,1,0:T(8,128)} %copy-done.2), channel_id=1, source_target_pairs={{0,1},{1,0},{2,3},{3,2},{4,5},{5,4},{6,7},{7,6},{8,9},{9,8},{10,11... | collective-permute-start | bytes 1179656 | tf_op jit(solution)/shard_map/ppermute | solution.py:256
  117.8 6.6 %collective-permute-start.5 = (f32[4,64,384]{2,1,0:T(8,128)S(1)}, f32[4,64,384]{2,1,0:T(8,128)S(1)}, u32[]{:S(2)}, u32[]{:S(2)}) collective-permute-start(f32[4,64,384]{2,1,0:T(8,128)S(1)} %get-tuple-element.58), channel_id=1, source_target_pairs={{0,1},{1,0},{2,3},{3,2},{4,5},{5,4},{6,7},{7,6},{8,9},{9,8},{10,11... | collective-permute-start | bytes 1179656 | tf_op jit(solution)/shard_map/ppermute | solution.py:256
  124.3 6.3 %copy-start.17 = (f32[4,64,384]{2,1,0:T(8,128)}, f32[4,64,384]{2,1,0:T(8,128)S(1)}, u32[]{:S(2)}) copy-start(f32[4,64,384]{2,1,0:T(8,128)S(1)} %collective-permute-done.4.refs_4_) | copy-start | bytes 1179652
  124.4 6.3 %copy-start.18 = (f32[4,64,384]{2,1,0:T(8,128)}, f32[4,64,384]{2,1,0:T(8,128)S(1)}, u32[]{:S(2)}) copy-start(f32[4,64,384]{2,1,0:T(8,128)S(1)} %collective-permute-done.5.refs_5_) | copy-start | bytes 1179652
  131.3 25.9 %copy-start.8 = (bf16[1,128,2560]{2,1,0:T(8,128)(2,1)S(1)}, bf16[1,128,2560]{2,1,0:T(8,128)(2,1)}, u32[]{:S(2)}) copy-start(bf16[1,128,2560]{2,1,0:T(8,128)(2,1)} %param.16) | copy-start | bytes 1966084
  146.6 39.0 %copy-start.15 = (f32[51]{0:T(128)S(1)}, f32[51]{0:T(128)}, u32[]{:S(2)}) copy-start(f32[51]{0:T(128)} %param.19) | copy-start | bytes 616
  146.6 10.6 %all-to-all-start.3 = ((bf16[8,2,64,128]{3,2,1,0:T(8,128)(2,1)}), bf16[8,2,64,128]{3,2,1,0:T(8,128)(2,1)S(1)}, u32[]{:S(2)}, u32[]{:S(2)}) async-start(bf16[8,2,64,128]{3,2,1,0:T(8,128)(2,1)} %bitcast.86), calls=%async_computation.3 | async-start | bytes 524288 | tf_op jit(solution)/shard_map/all_to_all | solution.py:276
  157.7 47.8 %copy-start.14 = (f32[128,64]{0,1:T(8,128)S(1)}, f32[128,64]{0,1:T(8,128)}, u32[]{:S(2)}) copy-start(f32[128,64]{0,1:T(8,128)} %param.14) | copy-start | bytes 98308
  158.6 37.1 %all-to-all-start.4 = ((bf16[16,64,128]{2,1,0:T(8,128)(2,1)}), bf16[16,64,128]{2,1,0:T(8,128)(2,1)S(1)}, u32[]{:S(2)}, u32[]{:S(2)}) async-start(bf16[16,64,128]{2,1,0:T(8,128)(2,1)} %bitcast.19), calls=%async_computation.4 | async-start | bytes 524288 | tf_op jit(solution)/shard_map/all_to_all | solution.py:282
  196.6 8.8 %all-to-all-start.5 = ((f32[4,64,128]{2,1,0:T(8,128)}), f32[4,64,128]{2,1,0:T(8,128)S(1)}, u32[]{:S(2)}, u32[]{:S(2)}) async-start(f32[4,64,128]{2,1,0:T(8,128)} %broadcast_in_dim.124), calls=%async_computation.5 | async-start | bytes 262144 | tf_op jit(solution)/shard_map/all_to_all | solution.py:216
  (7 other events, 6.6 us)
